TPU v7x, 256 devices: a whole 4x4x8 slice. The times are simulated.
256 devices in a mesh: px: 32 (over z, x), py: 8 (over y, core).
Axes of the slice: x: 4, y: 4, z: 8, core: 2. Of those that a mesh axis runs over, the one named last changes fastest.
Arguments:
- corr: float32 [3, 256, 256, 256], P(None, 'px', 'py'), may hold values from -6 to 6
- solute_pot: bfloat16 [3, 256, 256, 256], P(None, 'px', 'py'), may hold values from -8 to 8
- chi: float32 [3, 3, 2, 128, 256, 256], P(None, None, None, 'py', 'px'), may hold values from -1 to 2, as said below
- site_charge: float32 [3], replicated, may hold values from -1 to 1
- home_slab: int32 [8192, 1], P(('px', 'py')), may hold values from 0 to 31; in each aligned block of 32 rows (0 to 31, 32 to 63, ...) at most 4 rows name the same one
- brick_index: int32 [8192], P(('px', 'py')), may hold values from 0 to 127
- block_slot: int32 [256, 32], P(('px', 'py')), may hold values from 0 to 31, each once within a row
- basis_values: bfloat16 [8192, 512, 128], P(('px', 'py')), may hold values from -0.25 to 0.25
- fock_in: float32 [8192, 128, 128], P(('px', 'py')), may hold values from -6 to 6
Outputs:
- corr_next: float32 [3, 256, 256, 256], P(None, 'px', 'py')
- potential: float32 [256, 256, 256], P('px', 'py')
- fock_out: float32 [8192, 128, 128], P(('px', 'py'))
Inputs may be any that keep to these rules, and one draw needn't show every extreme that they name: Among the 32 fragments of one device at most 4 have the same home_slab, and in every draw some device has 4 fragments with one home_slab. `block_slot`: each row is a permutation of 0 to 31. chi at wave vector (kx, kz, ky) equals chi at ((-kx) mod 256, (-kz) mod 256, (-ky) mod 256).
All inputs are finite; a program needn't handle non-finite values.
Results may differ from a plain program's by a relative error of at most 0.0011.
Values may be sent and summed in bfloat16 or wider, within the bound.
A program may use at most 128 MiB of HBM per device.

v0:
```python
import jax
import jax.numpy as jnp
from jax import lax
from jax.sharding import PartitionSpec as P

BRICK = 8


SCREEN = 1.0
HIGH = lax.Precision.HIGHEST


def closure(corr, solute_pot):
    excess = corr - solute_pot.astype(jnp.float32)
    total_corr = jnp.where(excess > 0, excess, jnp.expm1(jnp.minimum(excess, 0.0)))
    return total_corr - corr


def wave_tables(length):
    index = jnp.arange(length, dtype=jnp.int32)
    phase = index[:, None] * index[None, :] % length
    angle = phase.astype(jnp.float32) * (2.0 * jnp.pi / length)
    return (jnp.cos(angle), jnp.sin(angle))


def signed_wave(index, length):
    shifted = (index + length // 2) % length - length // 2
    return shifted.astype(jnp.float32) * (2.0 * jnp.pi / length)


def rotate_pass(real_part, imag_part, cos_tab, sin_tab, orient, pattern):
    cos_re = jnp.einsum(pattern, real_part, cos_tab, precision=HIGH)
    sin_im = jnp.einsum(pattern, imag_part, sin_tab, precision=HIGH)
    cos_im = jnp.einsum(pattern, imag_part, cos_tab, precision=HIGH)
    sin_re = jnp.einsum(pattern, real_part, sin_tab, precision=HIGH)
    return (cos_re - orient * sin_im, cos_im + orient * sin_re)


def shards(
    corr, solute_pot, chi, site_charge, home_slab, brick_index, block_slot, basis_values, fock_in
):
    site_count, y_dev, z_dev, grid_len = corr.shape
    px_count = lax.axis_size("px")
    py_count = lax.axis_size("py")
    half_len = grid_len // 2
    half_dev = half_len // py_count
    kz_dev = grid_len // px_count
    column = lax.axis_index("py")
    cos_tab, sin_tab = wave_tables(grid_len)
    cells = y_dev * z_dev
    direct = closure(corr, solute_pot)
    flattened = direct.reshape(site_count, cells, grid_len)
    real_part = jnp.einsum("spx,xk->skp", flattened, cos_tab, precision=HIGH)
    imag_part = -jnp.einsum("spx,xk->skp", flattened, sin_tab, precision=HIGH)
    outgoing = jnp.stack([real_part, imag_part]).reshape(2, site_count, 2, half_len, cells)
    group_count = 2
    chi_local = chi.reshape(site_count, site_count, 2 * half_dev, kz_dev, grid_len)
    kx_ids = (
        jnp.arange(2, dtype=jnp.int32)[:, None] * half_len
        + column * half_dev
        + jnp.arange(half_dev, dtype=jnp.int32)[None, :]
    ).reshape(-1)
    kx_dev = group_count * half_dev
    sectioned = lax.all_to_all(outgoing, "py", split_axis=3, concat_axis=3, tiled=True)
    sectioned = sectioned.reshape(2, site_count, group_count, py_count, half_dev, y_dev, z_dev)
    real_part, imag_part = rotate_pass(
        sectioned[0],
        sectioned[1],
        cos_tab.reshape(py_count, z_dev, grid_len),
        sin_tab.reshape(py_count, z_dev, grid_len),
        -1.0,
        "sajkyz,jzm->smaky",
    )
    sectioned = jnp.stack([real_part, imag_part]).reshape(2, site_count, grid_len, kx_dev * y_dev)
    sectioned = lax.all_to_all(sectioned, "px", split_axis=2, concat_axis=2, tiled=True)
    sectioned = sectioned.reshape(2, site_count, px_count, kz_dev, kx_dev, y_dev)
    real_part, imag_part = rotate_pass(
        sectioned[0],
        sectioned[1],
        cos_tab.reshape(px_count, y_dev, grid_len),
        sin_tab.reshape(px_count, y_dev, grid_len),
        -1.0,
        "sjmky,jyn->skmn",
    )
    total_re = jnp.sum(chi_local * real_part[None], axis=1)
    total_im = jnp.sum(chi_local * imag_part[None], axis=1)
    ind_re = total_re - real_part
    ind_im = total_im - imag_part
    wave_x = signed_wave(kx_ids, grid_len)
    wave_z = signed_wave(
        lax.axis_index("px") * kz_dev + jnp.arange(kz_dev, dtype=jnp.int32), grid_len
    )
    wave_y = signed_wave(jnp.arange(grid_len, dtype=jnp.int32), grid_len)
    screened = (
        4.0
        * jnp.pi
        / (
            wave_x[:, None, None] ** 2
            + wave_z[None, :, None] ** 2
            + wave_y[None, None, :] ** 2
            + SCREEN * SCREEN
        )
    )
    charges = site_charge[:, None, None, None]
    pot_re = screened * jnp.sum(charges * total_re, axis=0)
    pot_im = screened * jnp.sum(charges * total_im, axis=0)
    field_re = jnp.concatenate([ind_re, pot_re[None]], axis=0)
    field_im = jnp.concatenate([ind_im, pot_im[None]], axis=0)
    field_count = field_re.shape[0]
    real_part, imag_part = rotate_pass(field_re, field_im, cos_tab, sin_tab, 1.0, "fkmn,ny->fykm")
    sectioned = jnp.stack([real_part, imag_part]).reshape(2, field_count, grid_len, kx_dev * kz_dev)
    sectioned = lax.all_to_all(sectioned, "px", split_axis=2, concat_axis=2, tiled=True)
    sectioned = sectioned.reshape(2, field_count, px_count, y_dev, kx_dev, kz_dev)
    real_part, imag_part = rotate_pass(
        sectioned[0],
        sectioned[1],
        cos_tab.reshape(px_count, kz_dev, grid_len),
        sin_tab.reshape(px_count, kz_dev, grid_len),
        1.0,
        "fjykm,jmz->fzyk",
    )
    sectioned = jnp.stack([real_part, imag_part]).reshape(2, field_count, grid_len, y_dev * kx_dev)
    sectioned = lax.all_to_all(sectioned, "py", split_axis=2, concat_axis=2, tiled=True)
    sectioned = sectioned.reshape(2, field_count, py_count, z_dev, y_dev, kx_dev)
    norm_factor = 1.0 / float(grid_len) ** 3
    last_cos = (
        cos_tab.reshape(2, py_count, half_dev, grid_len)
        .transpose(1, 0, 2, 3)
        .reshape(py_count, kx_dev, grid_len)
    )
    last_sin = (
        sin_tab.reshape(2, py_count, half_dev, grid_len)
        .transpose(1, 0, 2, 3)
        .reshape(py_count, kx_dev, grid_len)
    )
    out_re = jnp.einsum("fjzyk,jkx->fyzx", sectioned[0], last_cos, precision=HIGH) - jnp.einsum(
        "fjzyk,jkx->fyzx", sectioned[1], last_sin, precision=HIGH
    )
    corr_next = out_re[:site_count] * norm_factor
    potential = out_re[site_count] * norm_factor
    y_bricks = y_dev // BRICK
    z_bricks = z_dev // BRICK
    x_bricks = grid_len // BRICK
    brick_count = y_bricks * z_bricks * x_bricks
    brick_cells = BRICK * BRICK * BRICK
    bricks = potential.reshape(y_bricks, BRICK, z_bricks, BRICK, x_bricks, BRICK)
    bricks = (
        bricks.transpose(0, 2, 4, 1, 3, 5).reshape(brick_count, brick_cells).astype(jnp.bfloat16)
    )
    home_slot = home_slab[:, 0]
    frag_count = home_slot.shape[0]
    wanted = home_slot * brick_count + brick_index
    shard_rows = lax.all_gather(bricks, "px", axis=0, tiled=True)
    inside = (wanted >= 0) & (wanted < shard_rows.shape[0])
    picked = jnp.take(shard_rows, jnp.clip(wanted, 0, shard_rows.shape[0] - 1), axis=0)
    sampled = jnp.where(inside[:, None], picked, jnp.zeros((frag_count, brick_cells), jnp.bfloat16))
    weighted = (basis_values.astype(jnp.float32) * sampled.astype(jnp.float32)[:, :, None]).astype(
        jnp.bfloat16
    )
    embed = jnp.einsum("fcb,fcd->fbd", basis_values, weighted, preferred_element_type=jnp.float32)
    fock_out = fock_in.at[block_slot[0]].add(embed)
    return (corr_next, potential, fock_out)


def solution(mesh):
    return jax.shard_map(
        shards,
        mesh=mesh,
        in_specs=(
            P(None, "px", "py", None),
            P(None, "px", "py", None),
            P(None, None, None, "py", "px", None),
            P(),
            P(("px", "py"), None),
            P(("px", "py")),
            P(("px", "py"), None),
            P(("px", "py"), None, None),
            P(("px", "py"), None, None),
        ),
        out_specs=(P(None, "px", "py", None), P("px", "py", None), P(("px", "py"), None, None)),
        check_vma=False,
    )
```

profile of v0, /device:TPU:8, one launch (start us, length us, event | category | flops | bytes accessed | tf_op | source)
XLA Modules:
  0.0 513.6 jit_solution(1282041338182685207)
XLA Ops:
  16.6 5.7 %all-to-all-start = ((f32[2,3,2,128,256]{4,2,1,0,3:T(2,128)}), f32[2,3,2,128,256]{4,2,1,0,3:T(2,128)S(1)}, u32[]{:S(2)}, u32[]{:S(2)}) async-start(f32[2,3,2,128,256]{4,2,1,0,3:T(2,128)} %pad_maximum_fusion.2), calls=%async_computation | async-start | bytes 3145728 | tf_op jit(solution)/shard_map/all_to_all | solution.py:64
  22.3 20.1 %all-to-all-done = f32[2,3,2,128,256]{4,2,1,0,3:T(2,128)S(1)} async-done(((f32[2,3,2,128,256]{4,2,1,0,3:T(2,128)}), f32[2,3,2,128,256]{4,2,1,0,3:T(2,128)S(1)}, u32[]{:S(2)}, u32[]{:S(2)}) %all-to-all-start) | async-done | bytes 1572896 | tf_op jit(solution)/shard_map/all_to_all | solution.py:64
  49.9 5.3 %fusion.46 = f32[256,3,2,16,8]{0,3,4,2,1:T(8,128)S(1)} fusion(f32[3,2,8,16,8,32]{5,4,1,0,3,2:T(8,128)S(1)} %reshape.600, s32[8,32]{1,0:T(8,128)S(1)} %multiply_add_fusion.1), kind=kOutput, calls=%fused_computation.44 | convolution fusion | flops 605093888 | bytes 1573888 | tf_op jit(solution)/shard_map/sajkyz,jzm->smaky/dot_general | solution.py:33
  55.2 5.4 %fusion.40 = f32[256,3,2,16,8]{0,3,4,2,1:T(8,128)S(1)} fusion(f32[3,2,8,16,8,32]{5,4,1,0,3,2:T(8,128)S(1)} %copy-done.1, s32[8,32]{1,0:T(8,128)S(1)} %multiply_add_fusion.1), kind=kOutput, calls=%fused_computation.42 | convolution fusion | flops 605093888 | bytes 1573888 | tf_op jit(solution)/shard_map/sajkyz,jzm->smaky/dot_general | solution.py:35
  60.6 5.6 %fusion.62 = f32[3,256,2,16,8]{1,3,4,2,0:T(8,128)S(1)} fusion(f32[256,3,2,16,8]{0,3,4,2,1:T(8,128)S(1)} %fusion.46, f32[3,2,8,16,8,32]{5,4,1,0,3,2:T(8,128)S(1)} %copy-done.1, s32[8,32]{1,0:T(8,128)S(1)} %multiply_add_fusion.1), kind=kOutput, calls=%fused_computation.57 | convolution fusion | flops 605093888 | bytes 2360320 | tf_op jit(solution)/shard_map/sajkyz,jzm->smaky/dot_general | solution.py:32
  66.7 5.3 %fusion.59 = f32[3,256,2,16,8]{1,3,4,2,0:T(8,128)S(1)} fusion(f32[256,3,2,16,8]{0,3,4,2,1:T(8,128)S(1)} %fusion.40, f32[3,2,8,16,8,32]{5,4,1,0,3,2:T(8,128)S(1)} %reshape.600, s32[8,32]{1,0:T(8,128)S(1)} %multiply_add_fusion.1), kind=kOutput, calls=%fused_computation.56 | convolution fusion | flops 605093888 | bytes 2360320 | tf_op jit(solution)/shard_map/sajkyz,jzm->smaky/dot_general | solution.py:34
  74.6 10.9 %all-to-all-start.1 = ((f32[2,3,256,256]{3,0,1,2:T(2,128)}), f32[2,3,256,256]{3,0,1,2:T(2,128)S(1)}, u32[]{:S(2)}, u32[]{:S(2)}) async-start(f32[2,3,256,256]{3,0,1,2:T(2,128)} %copy.105), calls=%async_computation.1 | async-start | bytes 3145728 | tf_op jit(solution)/shard_map/all_to_all | solution.py:75
  85.9 38.6 %all-to-all-done.1 = f32[2,3,256,256]{3,0,1,2:T(2,128)S(1)} async-done(((f32[2,3,256,256]{3,0,1,2:T(2,128)}), f32[2,3,256,256]{3,0,1,2:T(2,128)S(1)}, u32[]{:S(2)}, u32[]{:S(2)}) %all-to-all-start.1) | async-done | bytes 1572896 | tf_op jit(solution)/shard_map/all_to_all | solution.py:75
  124.5 5.3 %slice_reduce_fusion.1 = (f32[3,256,256]{2,0,1:T(4,128)}, f32[3,256,256]{2,0,1:T(4,128)S(1)}) fusion(f32[2,3,256,256]{3,0,1,2:T(2,128)S(1)} %all-to-all-done.1), kind=kLoop, calls=%fused_computation.67 | loop fusion | bytes 3145728 | tf_op jit(solution)/shard_map/slice | solution.py:78
  129.8 8.7 %reshape.602 = f32[3,32,8,32,8]{4,3,0,2,1:T(8,128)} reshape(f32[3,256,256]{2,0,1:T(4,128)S(1)} %get-tuple-element.6) | data formatting | bytes 1572864 | tf_op jit(solution)/shard_map/squeeze | solution.py:79
  138.5 9.6 %copy.109 = f32[3,32,8,32,8]{1,3,4,2,0:T(8,128)S(1)} copy(f32[3,32,8,32,8]{4,3,0,2,1:T(8,128)} %reshape.602) | data formatting | bytes 1572864 | tf_op jit(solution)/shard_map/squeeze | solution.py:79
  148.1 10.0 %reshape.601 = f32[3,32,8,32,8]{4,3,0,2,1:T(8,128)} reshape(f32[3,256,256]{2,0,1:T(4,128)} %get-tuple-element.5) | data formatting | bytes 1572864 | tf_op jit(solution)/shard_map/squeeze | solution.py:78
  158.1 10.8 %copy.107 = f32[3,32,8,32,8]{1,3,4,2,0:T(8,128)} copy(f32[3,32,8,32,8]{4,3,0,2,1:T(8,128)} %reshape.601) | data formatting | bytes 1572864 | tf_op jit(solution)/shard_map/squeeze | solution.py:78
  169.0 4.7 convolution_bitcast_fusion.5
  173.7 4.8 convolution_bitcast_fusion.7
  178.5 5.0 fusion.58
  184.0 4.8 fusion.57
  202.8 55.2 %all_to_all.20 = f32[2,4,256,256]{3,1,0,2:T(4,128)S(1)} all-to-all(f32[2,4,256,256]{3,1,0,2:T(4,128)} %copy.120), channel_id=1, replica_groups=mesh['px'=32,'py'=8] {'px'}, dimensions={2} | all-to-all | bytes 4194304 | tf_op jit(solution)/shard_map/all_to_all | solution.py:112
  258.4 11.1 %reshape.604 = f32[4,32,8,32,8]{4,3,0,2,1:T(8,128)} reshape(f32[1,4,256,256]{3,1,0,2:T(4,128)S(1)} %get-tuple-element.13) | data formatting | bytes 2097152 | tf_op jit(solution)/shard_map/squeeze | solution.py:116
  269.5 13.7 %copy.124 = f32[4,32,8,32,8]{1,3,4,2,0:T(8,128)} copy(f32[4,32,8,32,8]{4,3,0,2,1:T(8,128)} %reshape.604) | data formatting | bytes 2097152 | tf_op jit(solution)/shard_map/squeeze | solution.py:116
  283.1 9.4 %convolution_bitcast_fusion.2 = f32[256,4,8,32]{0,3,2,1:T(8,128)} fusion(f32[4,32,8,32,8]{1,3,4,2,0:T(8,128)} %copy.124, s32[32,8]{0,1:T(8,128)S(1)} %multiply_add_fusion.2), kind=kOutput, calls=%fused_computation.29 | convolution fusion | flops 806223872 | bytes 2098176 | tf_op jit(solution)/shard_map/fjykm,jmz->fzyk/dot_general | solution.py:33
  292.6 11.0 %reshape.603 = f32[4,32,8,32,8]{4,3,0,2,1:T(8,128)} reshape(f32[1,4,256,256]{3,1,0,2:T(4,128)S(1)} %get-tuple-element.14) | data formatting | bytes 2097152 | tf_op jit(solution)/shard_map/squeeze | solution.py:115
  303.6 13.7 %copy.122 = f32[4,32,8,32,8]{1,3,4,2,0:T(8,128)} copy(f32[4,32,8,32,8]{4,3,0,2,1:T(8,128)} %reshape.603) | data formatting | bytes 2097152 | tf_op jit(solution)/shard_map/squeeze | solution.py:115
  317.3 9.0 %convolution_bitcast_fusion = f32[256,4,8,32]{0,3,2,1:T(8,128)S(1)} fusion(f32[4,32,8,32,8]{1,3,4,2,0:T(8,128)} %copy.122, s32[32,8]{0,1:T(8,128)S(1)} %multiply_add_fusion.2), kind=kOutput, calls=%fused_computation.27 | convolution fusion | flops 806223872 | bytes 2098176 | tf_op jit(solution)/shard_map/fjykm,jmz->fzyk/dot_general | solution.py:35
  326.4 6.0 %fusion.23 = f32[256,4,8,32]{0,3,2,1:T(8,128)S(1)} fusion(f32[256,4,8,32]{0,3,2,1:T(8,128)S(1)} %copy-done.6, f32[4,32,8,32,8]{1,3,4,2,0:T(8,128)S(1)} %copy-done, s32[32,8]{0,1:T(8,128)S(1)} %multiply_add_fusion.2), kind=kOutput, calls=%fused_computation.35 | convolution fusion | flops 806486016 | bytes 3146752 | tf_op jit(solution)/shard_map/fjykm,jmz->fzyk/dot_general | solution.py:32
  332.8 8.7 %fusion.24 = f32[256,4,8,32]{0,3,2,1:T(8,128)S(1)} fusion(f32[256,4,8,32]{0,3,2,1:T(8,128)S(1)} %convolution_bitcast_fusion, f32[4,32,8,32,8]{1,3,4,2,0:T(8,128)} %copy.124, s32[32,8]{0,1:T(8,128)S(1)} %multiply_add_fusion.2), kind=kOutput, calls=%fused_computation.36 | convolution fusion | flops 806486016 | bytes 3146752 | tf_op jit(solution)/shard_map/fjykm,jmz->fzyk/dot_general | solution.py:34
  343.7 5.0 all-to-all-start.3
  350.9 23.5 %all-to-all-done.3 = f32[2,4,256,256]{3,1,0,2:T(4,128)S(1)} async-done(((f32[2,4,256,256]{3,1,0,2:T(4,128)}), f32[2,4,256,256]{3,1,0,2:T(4,128)S(1)}, u32[]{:S(2)}, u32[]{:S(2)}) %all-to-all-start.3) | async-done | bytes 2097184 | tf_op jit(solution)/shard_map/all_to_all | solution.py:123
  382.2 9.9 %fusion.15 = f32[256,4,32,8]{0,2,3,1:T(8,128)S(1)} fusion(f32[8,32,256,1,1]{2,1,0,4,3:T(8,128)S(1)} %bitcast.250, f32[4,8,32,8,32]{4,3,0,2,1:T(8,128)} %reshape.597), kind=kOutput, calls=%fused_computation.25 | convolution fusion | flops 805306368 | bytes 2359296 | tf_op jit(solution)/shard_map/fjzyk,jkx->fyzx/dot_general | solution.py:136
  392.1 7.6 %fusion.28 = f32[4,8,32,256]{3,2,1,0:T(8,128)S(1)} fusion(f32[256,4,32,8]{0,2,3,1:T(8,128)S(1)} %fusion.15, f32[8,32,256,1,1]{2,1,0,4,3:T(8,128)S(1)} %bitcast.249, f32[4,8,32,8,32]{4,3,0,2,1:T(8,128)S(1)} %copy-done.3), kind=kOutput, calls=%fused_computation.38 | convolution fusion | flops 805568512 | bytes 3407872 | tf_op jit(solution)/shard_map/fjzyk,jkx->fyzx/dot_general | solution.py:136
  407.7 77.0 %all-gather.2.cloned.1.call-done = bf16[4096,512]{1,0:T(8,128)(2,1)} async-done(((bf16[128,512]{1,0:T(8,128)(2,1)}), bf16[4096,512]{1,0:T(8,128)(2,1)}) %all-gather.2.cloned.1.call-update) | async-done | bytes 4194320 | tf_op jit(solution)/shard_map/all_gather | solution.py:153
  488.2 9.2 %fusion.14 = f32[32,128,128]{1,2,0:T(8,128)} fusion(bf16[32,512,128]{2,1,0:T(8,128)(2,1)} %param.16, f32[32,512]{1,0:T(8,128)S(1)} %select_convert_fusion), kind=kOutput, calls=%fused_computation.22 | convolution fusion | flops 543162368 | bytes 6356992 | tf_op jit(solution)/shard_map/fcb,fcd->fbd/dot_general | solution.py:160
  (94 shorter events, 68.1 us)
Async XLA Ops:
  7.2 1.1 copy-start.9
  7.2 1.2 copy-start.10
  16.6 25.8 %all-to-all-start = ((f32[2,3,2,128,256]{4,2,1,0,3:T(2,128)}), f32[2,3,2,128,256]{4,2,1,0,3:T(2,128)S(1)}, u32[]{:S(2)}, u32[]{:S(2)}) async-start(f32[2,3,2,128,256]{4,2,1,0,3:T(2,128)} %pad_maximum_fusion.2), calls=%async_computation | async-start | bytes 3145728 | tf_op jit(solution)/shard_map/all_to_all | solution.py:64
  49.9 5.3 %copy-start.1 = (f32[3,2,8,16,8,32]{5,4,1,0,3,2:T(8,128)S(1)}, f32[3,2,8,16,8,32]{5,4,1,0,3,2:T(8,128)}, u32[]{:S(2)}) copy-start(f32[3,2,8,16,8,32]{5,4,1,0,3,2:T(8,128)} %reshape.599) | copy-start | bytes 2359300
  74.6 49.8 %all-to-all-start.1 = ((f32[2,3,256,256]{3,0,1,2:T(2,128)}), f32[2,3,256,256]{3,0,1,2:T(2,128)S(1)}, u32[]{:S(2)}, u32[]{:S(2)}) async-start(f32[2,3,256,256]{3,0,1,2:T(2,128)} %copy.105), calls=%async_computation.1 | async-start | bytes 3145728 | tf_op jit(solution)/shard_map/all_to_all | solution.py:75
  169.0 4.7 copy-start.2
  184.0 5.2 %copy-start.7 = (f32[3,3,2,16,8,256]{5,4,3,2,1,0:T(8,128)S(1)}, f32[3,3,2,16,8,256]{5,4,3,2,1,0:T(8,128)}, u32[]{:S(2)}) copy-start(f32[3,3,2,16,8,256]{5,4,3,2,1,0:T(8,128)} %param.11) | copy-start | bytes 7077892
  189.7 0.7 copy-start.11
  317.3 9.0 %copy-start = (f32[4,32,8,32,8]{1,3,4,2,0:T(8,128)S(1)}, f32[4,32,8,32,8]{1,3,4,2,0:T(8,128)}, u32[]{:S(2)}) copy-start(f32[4,32,8,32,8]{1,3,4,2,0:T(8,128)} %copy.122) | copy-start | bytes 3145732
  317.3 9.0 %copy-start.6 = (f32[256,4,8,32]{0,3,2,1:T(8,128)S(1)}, f32[256,4,8,32]{0,3,2,1:T(8,128)}, u32[]{:S(2)}) copy-start(f32[256,4,8,32]{0,3,2,1:T(8,128)} %convolution_bitcast_fusion.2) | copy-start | bytes 3145732
  343.7 30.7 %all-to-all-start.3 = ((f32[2,4,256,256]{3,1,0,2:T(4,128)}), f32[2,4,256,256]{3,1,0,2:T(4,128)S(1)}, u32[]{:S(2)}, u32[]{:S(2)}) async-start(f32[2,4,256,256]{3,1,0,2:T(4,128)} %pad_maximum_fusion.1), calls=%async_computation.3 | async-start | bytes 4194304 | tf_op jit(solution)/shard_map/all_to_all | solution.py:123
  348.7 136.1 %all-gather.2.cloned.1.call-start = ((), (), s32[]{:S(2)}) async-start(), calls=%async_computation.4 | async-start | bytes 4325376 | tf_op jit(solution)/shard_map/all_gather | solution.py:153
  379.6 2.6 copy-start.8
  382.2 9.9 %copy-start.3 = (f32[4,8,32,8,32]{4,3,0,2,1:T(8,128)S(1)}, f32[4,8,32,8,32]{4,3,0,2,1:T(8,128)}, u32[]{:S(2)}) copy-start(f32[4,8,32,8,32]{4,3,0,2,1:T(8,128)} %reshape.598) | copy-start | bytes 3145732
  399.7 7.0 %copy-start.12 = (s32[32]{0:T(128)S(1)}, s32[32]{0:T(128)}, u32[]{:S(2)}) copy-start(s32[32]{0:T(128)} %param.14) | copy-start | bytes 388
  399.7 7.0 %copy-start.13 = (s32[32,1]{0,1:T(1,128)S(1)}, s32[32,1]{0,1:T(1,128)}, u32[]{:S(2)}) copy-start(s32[32,1]{0,1:T(1,128)} %param.13) | copy-start | bytes 388
  399.7 7.1 %copy-start.14 = (s32[1,32]{1,0:T(1,128)S(1)}, s32[1,32]{1,0:T(1,128)}, u32[]{:S(2)}) copy-start(s32[1,32]{1,0:T(1,128)} %param.15) | copy-start | bytes 388
  497.4 3.1 copy-start.5
  505.2 1.3 copy-start.4
Sparse Core Ops, SparseCore 0:
  406.8 77.8 all-gather.1
where the time goes:
time: 522 us; the launch traced here: 514 us
  waiting for transfers between devices  159 us (30%)
  local copies, waits for them, and re-layouts  135 us (26%)
  matrix products  114 us (22%)
  blocking collectives  55.2 us (11%)
  starting transfers between devices  21.6 us (4%)
  between operations  14.8 us (3%)
  other arithmetic  14.3 us (3%)
    all_gather x1, waiting for transfers between devices, shards(): shard_rows = lax.all_gather(bricks, 'px', axis=0, tiled=True)  77 us
    all_to_all x1, blocking collectives, shards(): lax.all_to_all(sectioned, 'px', split_axis=2, concat_axis=2, tiled=True)  55.2 us
    squeeze x6, local copies, waits for them, and re-layouts, shards(): sectioned[0]  53 us
    squeeze x6, local copies, waits for them, and re-layouts, shards(): sectioned[1]  47.8 us
    all_to_all x1, waiting for transfers between devices, shards(): lax.all_to_all(sectioned, 'px', split_axis=2, concat_axis=2, tiled=True)  38.6 us
    all_to_all x1, waiting for transfers between devices, shards(): lax.all_to_all(sectioned, 'py', split_axis=2, concat_axis=2, tiled=True)  23.5 us
    dot_general x4, matrix products, rotate_pass(): sin_re = jnp.einsum(pattern, real_part, sin_tab, precision=HIGH)  21.5 us
    dot_general x4, matrix products, rotate_pass(): sin_im = jnp.einsum(pattern, imag_part, sin_tab, precision=HIGH)  21.5 us
  transfers between devices with their start and end apart: 4, of which 4 were waited for; matrix products, arithmetic and copies ran while one was open for 1% of the time, Pallas kernels for 0%

commit v1 on v0

v1 whole, which is shorter than its diff:
```python
import functools
import jax
import jax.numpy as jnp
import numpy as np
from jax import lax
from jax.experimental import pallas as pl
from jax.experimental.pallas import tpu as pltpu
from jax.sharding import PartitionSpec as P

BRICK = 8
MOST = 4
N = 256
PX = 32
PY = 8
SITES = 3
FIELDS = 4
R = 16
MESH = pl.DeviceIdType.MESH
F32 = jnp.float32
BF16 = jnp.bfloat16
WIRE = jnp.float32


def split(values):
    high = values.astype(BF16)
    return high, (values - high.astype(F32)).astype(BF16)


def np_split(values):
    high = values.astype(np.float32).astype(BF16)
    low = (values - high.astype(np.float64)).astype(np.float32).astype(BF16)
    return high, low


def tables():
    index = np.arange(N)
    angle = (index[:, None] * index[None, :] % N) * (2.0 * np.pi / N)
    cos, sin = np.cos(angle), np.sin(angle)
    half_re = cos[:, : N // 2].copy()
    half_im = -sin[:, : N // 2]
    half_im[:, 0] = cos[:, N // 2]
    halves = np.stack([half_re.reshape(N, PY, R), half_im.reshape(N, PY, R)], axis=2)
    spread = np.broadcast_to(halves[:, :, :, None, :], (N, PY, 2, FIELDS, R))
    spread = spread.reshape(N, PY * 128)
    return np_split(spread) + np_split(cos) + np_split(sin)


def encode(values):
    return values.astype(WIRE)


def decode(values):
    return values.astype(F32)


def dot(left, right):
    return jnp.dot(left, right, preferred_element_type=F32)


def dot_nt(left, right):
    return lax.dot_general(left, right, (((1,), (1,)), ((), ())), preferred_element_type=F32)


def dot3(product, left, right):
    return product(left[0], right[0]) + product(left[0], right[1]) + product(left[1], right[0])


def closure(corr, solute_pot):
    excess = corr - solute_pot.astype(F32)
    low = jnp.minimum(excess, 0.0)
    series = jnp.full_like(low, 1.0 / 362880.0)
    for denominator in (40320.0, 5040.0, 720.0, 120.0, 24.0, 6.0, 2.0, 1.0):
        series = series * low + 1.0 / denominator
    grown = jnp.where(low > -0.5, series * low, jnp.exp(low) - 1.0)
    return jnp.where(excess > 0, excess, grown) - corr


def field_kernel(
    corr_ref, pot_ref, chi_ref, charge_ref, xh_ref, xl_ref, ch_ref, cl_ref, sh_ref, sl_ref,
    corr_out, potential_out,
    chi0, chi1, s1, b1, s2, b2, ys, s3, b3, s4, b4,
    chi_sem, send1, recv1, send2, recv2, send3, recv3, send4, recv4,
):
    px = lax.axis_index("px")
    py = lax.axis_index("py")
    barrier = pltpu.get_barrier_semaphore()

    def greet_px(step, carry):
        pl.semaphore_signal(barrier, inc=1, device_id=(lax.rem(px + step, PX), py), device_id_type=MESH)
        return carry

    def greet_py(step, carry):
        pl.semaphore_signal(barrier, inc=1, device_id=(px, lax.rem(py + step, PY)), device_id_type=MESH)
        return carry

    lax.fori_loop(1, PX, greet_px, 0)
    lax.fori_loop(1, PY, greet_py, 0)
    chi_copy0 = pltpu.make_async_copy(chi_ref.at[:, :, 0], chi0, chi_sem.at[0])
    chi_copy1 = pltpu.make_async_copy(chi_ref.at[:, :, 1, 0], chi1, chi_sem.at[1])
    chi_copy0.start()
    chi_copy1.start()

    lane = lax.broadcasted_iota(jnp.int32, (1, 128), 1)
    lane_re = lane < 64
    lane_field = lax.rem(lane // R, FIELDS)
    lane_spec = (lax.rem(lane, R) == 0) & (py == 0)

    lane_site = jnp.concatenate([lane_field, lane_field], axis=1)

    def x_forward(yp, carry):
        parts = []
        for site in range(SITES):
            rows = closure(corr_ref[site, pl.ds(2 * yp, 2)], pot_ref[site, pl.ds(2 * yp, 2)])
            parts.append(rows.reshape(64, N))
        data = split(jnp.concatenate(parts, axis=0))
        for pair in range(PY // 2):
            wide = dot3(dot, data, (xh_ref[:, 256 * pair:256 * pair + 256], xl_ref[:, 256 * pair:256 * pair + 256]))
            rows = jnp.where(lane_site == 0, wide[0:64], jnp.where(lane_site == 1, wide[64:128], wide[128:192]))
            rows = encode(jnp.where(lane_site == 3, 0.0, rows))
            s1[2 * pair, pl.ds(2 * yp, 2)] = rows[:, 0:128].reshape(2, 32, 128)
            s1[2 * pair + 1, pl.ds(2 * yp, 2)] = rows[:, 128:256].reshape(2, 32, 128)

        @pl.when(yp == 0)
        def _():
            pl.semaphore_wait(barrier, PX + PY - 2)

        pltpu.make_async_copy(
            s1.at[py, pl.ds(2 * yp, 2)], b1.at[pl.ds(2 * yp, 2), pl.ds(32 * py, 32)], recv1.at[yp]
        ).start()

        def send(step, inner):
            other = lax.rem(py + step, PY)
            pltpu.make_async_remote_copy(
                src_ref=s1.at[other, pl.ds(2 * yp, 2)],
                dst_ref=b1.at[pl.ds(2 * yp, 2), pl.ds(32 * py, 32)],
                send_sem=send1.at[yp], recv_sem=recv1.at[yp],
                device_id=(px, other), device_id_type=MESH,
            ).start()
            return inner

        return lax.fori_loop(1, PY, send, carry)

    lax.fori_loop(0, 4, x_forward, 0)

    cos = (ch_ref[...], cl_ref[...])
    sin = (sh_ref[...], sl_ref[...])
    wave = lax.broadcasted_iota(jnp.int32, (N, 1), 0)
    wave_edge = (wave == 0) | (wave == N // 2)
    wave_low = wave < N // 2
    wave_high = wave > N // 2

    def z_forward(yp, carry):
        chunk = b1.at[pl.ds(2 * yp, 2)]
        pltpu.make_async_copy(chunk, chunk, recv1.at[yp]).wait()
        data = split(jnp.concatenate([decode(b1[2 * yp]), decode(b1[2 * yp + 1])], axis=1))
        cos_data = dot3(dot, cos, data)
        sin_data = dot3(dot, sin, data)
        halves = []
        for u in range(2):
            cd = cos_data[:, 128 * u:128 * u + 128]
            sd = sin_data[:, 128 * u:128 * u + 128]
            cd_turn = pltpu.roll(cd, 64, 1)
            sd_turn = pltpu.roll(sd, 64, 1)
            usual = jnp.where(lane_re, cd + sd_turn, cd - sd_turn)
            packed_re = jnp.where(wave_high, cd_turn, cd)
            packed_im = jnp.where(wave_edge, cd, jnp.where(wave_low, -sd_turn, -sd))
            packed = jnp.where(lane_re, packed_re, packed_im)
            halves.append(jnp.where(lane_spec, packed, usual).reshape(PX, 8, 128))
        s2[:, yp] = encode(jnp.concatenate(halves, axis=1))
        pltpu.make_async_copy(s2.at[px, yp], b2.at[px, yp], recv2.at[yp]).start()

        def send(step, inner):
            other = lax.rem(px + step, PX)
            pltpu.make_async_remote_copy(
                src_ref=s2.at[other, yp], dst_ref=b2.at[px, yp],
                send_sem=send2.at[yp], recv_sem=recv2.at[yp],
                device_id=(other, py), device_id_type=MESH,
            ).start()
            return inner

        return lax.fori_loop(1, PX, send, carry)

    lax.fori_loop(0, 4, z_forward, 0)

    def collect(buffer, sem):
        def body(part, carry):
            chunk = buffer.at[:, part]
            pltpu.make_async_copy(chunk, chunk, sem.at[part]).wait()

            def place(source, inner):
                start = pl.multiple_of(source * 64 + part * 16, 16)
                ys[pl.ds(start, 16), :] = decode(buffer[source, part])
                return inner

            return lax.fori_loop(0, PX, place, carry)

        lax.fori_loop(0, 4, body, 0)

    collect(b2, recv2)
    chi_copy0.wait()
    chi_copy1.wait()

    row = lax.broadcasted_iota(jnp.int32, (R, 1), 0)
    first = (row == 0) & (py == 0)
    wave_y = lax.broadcasted_iota(jnp.int32, (1, N), 1)
    unit = 2.0 * np.pi / N

    def signed_square(index):
        shifted = (lax.rem(index + N // 2, N) - N // 2).astype(F32) * unit
        return shifted * shifted

    square_y = signed_square(wave_y)
    scale = jnp.where(first, 2.0 ** -24, 2.0 ** -23)

    def mix(chi_of, x_re, x_im, screened):
        out_re, out_im = [], []
        pot_re = pot_im = 0.0
        for a in range(SITES):
            t_re = t_im = 0.0
            for b in range(SITES):
                factor = chi_of(a, b)
                t_re = t_re + factor * x_re[b]
                t_im = t_im + factor * x_im[b]
            out_re.append((t_re - x_re[a]) * scale)
            out_im.append((t_im - x_im[a]) * scale)
            pot_re = pot_re + charge_ref[a] * t_re
            pot_im = pot_im + charge_ref[a] * t_im
        out_re.append(pot_re * (screened * scale))
        out_im.append(pot_im * (screened * scale))
        return out_re, out_im

    def y_both(kp, carry):
        plain, turned = [], []
        rows = jnp.concatenate(
            [ys[pl.ds(2 * kp + u, N, stride=8), :].T for u in range(2)], axis=0
        )
        data = split(rows)
        cos_data = dot3(dot, data, cos)
        sin_data = dot3(dot, data, sin)
        for u in range(2):
            kz = 2 * kp + u
            kz_all = px * 8 + kz
            base = 128 * u
            pick = lambda array, c, s: array[base + 64 * c + 16 * s:base + 64 * c + 16 * s + 16]
            c_re = [pick(cos_data, 0, s) for s in range(SITES)]
            c_im = [pick(cos_data, 1, s) for s in range(SITES)]
            s_re = [pick(sin_data, 0, s) for s in range(SITES)]
            s_im = [pick(sin_data, 1, s) for s in range(SITES)]
            x_re = [c_re[s] + s_im[s] for s in range(SITES)]
            x_im = [c_im[s] - s_re[s] for s in range(SITES)]
            upper = first & (kz_all > N // 2)
            kx = jnp.where(upper, N // 2, py * R + row)
            square_z = signed_square(jnp.full((1, 1), kz_all, jnp.int32))
            rest = square_z + square_y + 1.0
            screened = (4.0 * np.pi) / (signed_square(kx) + rest)
            chi_of = lambda a, b: jnp.where(upper, chi1[a, b, pl.ds(kz, 1), :], chi0[a, b, :, kz, :])
            if u == 0:
                edge = first & ((kz_all == 0) | (kz_all == N // 2))
                b_re = [c_im[s] for s in range(SITES)]
                b_im = [-s_im[s] for s in range(SITES)]
                x_re = [jnp.where(edge, c_re[s], x_re[s]) for s in range(SITES)]
                x_im = [jnp.where(edge, -s_re[s], x_im[s]) for s in range(SITES)]
                f_re, f_im = mix(chi_of, x_re, x_im, screened)
                screened = (4.0 * np.pi) / (np.pi ** 2 + rest)
                g_re, g_im = mix(lambda a, b: chi1[a, b, pl.ds(kz, 1), :], b_re, b_im, screened)
                plain += f_re + [jnp.where(edge, g_re[f], f_im[f]) for f in range(FIELDS)]
                turned += [-value for value in f_im]
                turned += [jnp.where(edge, -g_im[f], f_re[f]) for f in range(FIELDS)]
            else:
                f_re, f_im = mix(chi_of, x_re, x_im, screened)
                plain += f_re + f_im
                turned += [-value for value in f_im] + f_re
        plain = split(jnp.concatenate(plain, axis=0))
        turned = split(jnp.concatenate(turned, axis=0))
        back = dot3(dot_nt, cos, plain) + dot3(dot_nt, sin, turned)
        s3[:, kp] = encode(
            jnp.concatenate([back[:, 128 * u:128 * u + 128].reshape(PX, 8, 128) for u in range(2)], axis=1)
        )
        pltpu.make_async_copy(s3.at[px, kp], b3.at[px, kp], recv3.at[kp]).start()

        def send(step, inner):
            other = lax.rem(px + step, PX)
            pltpu.make_async_remote_copy(
                src_ref=s3.at[other, kp], dst_ref=b3.at[px, kp],
                send_sem=send3.at[kp], recv_sem=recv3.at[kp],
                device_id=(other, py), device_id_type=MESH,
            ).start()
            return inner

        return lax.fori_loop(1, PX, send, carry)

    lax.fori_loop(0, 4, y_both, 0)

    collect(b3, recv3)

    def z_backward(yp, carry):
        plain, turned = [], []
        for u in range(2):
            data = ys[pl.ds(2 * yp + u, N, stride=8), :]
            turn = pltpu.roll(data, 64, 1)
            packed_re = jnp.where(wave_edge, data, jnp.where(wave_low, data + data, 0.0))
            packed_im = jnp.where(wave_edge, data, jnp.where(wave_low, 0.0, turn + turn))
            other_re = jnp.where(wave_low & ~wave_edge, -2.0 * turn, 0.0)
            other_im = jnp.where(wave_high, -2.0 * data, 0.0)
            plain.append(jnp.where(lane_spec, jnp.where(lane_re, packed_re, packed_im), data))
            turned.append(jnp.where(
                lane_spec, jnp.where(lane_re, other_re, other_im), jnp.where(lane_re, -turn, turn)
            ))
        plain = split(jnp.concatenate(plain, axis=1))
        turned = split(jnp.concatenate(turned, axis=1))
        back = encode(dot3(dot, cos, plain) + dot3(dot, sin, turned))
        s4[2 * yp] = back[:, 0:128]
        s4[2 * yp + 1] = back[:, 128:256]
        pltpu.make_async_copy(
            s4.at[pl.ds(2 * yp, 2), pl.ds(32 * py, 32)], b4.at[py, pl.ds(2 * yp, 2)], recv4.at[yp]
        ).start()

        def send(step, inner):
            other = lax.rem(py + step, PY)
            pltpu.make_async_remote_copy(
                src_ref=s4.at[pl.ds(2 * yp, 2), pl.ds(32 * other, 32)],
                dst_ref=b4.at[py, pl.ds(2 * yp, 2)],
                send_sem=send4.at[yp], recv_sem=recv4.at[yp],
                device_id=(px, other), device_id_type=MESH,
            ).start()
            return inner

        return lax.fori_loop(1, PY, send, carry)

    lax.fori_loop(0, 4, z_backward, 0)

    def x_backward(yp, carry):
        chunk = b4.at[:, pl.ds(2 * yp, 2)]
        pltpu.make_async_copy(chunk, chunk, recv4.at[yp]).wait()
        rows = jnp.concatenate(
            [decode(b4[j, pl.ds(2 * yp, 2)]).reshape(64, 128) for j in range(PY)], axis=1
        )
        field = jnp.concatenate([lane_field] * PY, axis=1)
        data = split(jnp.concatenate([jnp.where(field == f, rows, 0.0) for f in range(FIELDS)], axis=0))
        back = dot3(dot_nt, data, (xh_ref[...], xl_ref[...]))
        for f in range(SITES):
            corr_out[f, pl.ds(2 * yp, 2)] = back[64 * f:64 * f + 64].reshape(2, 32, N)
        potential_out[pl.ds(2 * yp, 2)] = back[192:256].reshape(2, 32, N)
        return carry

    lax.fori_loop(0, 4, x_backward, 0)

    for part in range(4):
        sent = s1.at[pl.ds(0, PY - 1), pl.ds(0, 2)]
        pltpu.make_async_copy(sent, sent, send1.at[part]).wait()
        sent = s2.at[pl.ds(0, PX - 1), 0]
        pltpu.make_async_copy(sent, sent, send2.at[part]).wait()
        pltpu.make_async_copy(sent, sent, send3.at[part]).wait()
        sent = s4.at[pl.ds(0, 2), pl.ds(0, 32 * (PY - 1))]
        pltpu.make_async_copy(sent, sent, send4.at[part]).wait()


def fields(corr, solute_pot, chi, site_charge):
    vmem = pl.BlockSpec(memory_space=pltpu.VMEM)
    dma = pltpu.SemaphoreType.DMA((4,))
    return pl.pallas_call(
        field_kernel,
        name="fields",
        out_shape=(
            jax.ShapeDtypeStruct((SITES, 8, 32, N), F32),
            jax.ShapeDtypeStruct((8, 32, N), F32),
        ),
        in_specs=[vmem, vmem, pl.BlockSpec(memory_space=pl.ANY), pl.BlockSpec(memory_space=pltpu.SMEM)] + [vmem] * 6,
        out_specs=(vmem, vmem),
        scratch_shapes=[
            pltpu.VMEM((SITES, SITES, R, 8, N), F32),
            pltpu.VMEM((SITES, SITES, 8, N), F32),
            pltpu.VMEM((PY, 8, 32, 128), WIRE),
            pltpu.VMEM((8, N, 128), WIRE),
            pltpu.VMEM((PX, 4, 16, 128), WIRE),
            pltpu.VMEM((PX, 4, 16, 128), WIRE),
            pltpu.VMEM((PX * 64, 128), F32),
            pltpu.VMEM((PX, 4, 16, 128), WIRE),
            pltpu.VMEM((PX, 4, 16, 128), WIRE),
            pltpu.VMEM((8, N, 128), WIRE),
            pltpu.VMEM((PY, 8, 32, 128), WIRE),
            pltpu.SemaphoreType.DMA((2,)),
        ] + [dma] * 8,
        compiler_params=pltpu.CompilerParams(
            collective_id=0, has_side_effects=True, vmem_limit_bytes=40 * 2**20
        ),
    )(corr, solute_pot, chi, site_charge, *[jnp.asarray(table) for table in tables()])


def shards(
    corr, solute_pot, chi, site_charge, home_slab, brick_index, block_slot, basis_values, fock_in
):
    home = home_slab[:, 0]
    frags = home.shape[0]
    same = home[:, None] == home[None, :]
    earlier = jnp.arange(frags)[None, :] < jnp.arange(frags)[:, None]
    place = jnp.sum((same & earlier).astype(jnp.int32), axis=1)
    wanted = home * MOST + place
    asked = jnp.zeros((PX * MOST,), jnp.int32).at[wanted].set(brick_index)
    asked = lax.all_to_all(asked, "px", split_axis=0, concat_axis=0, tiled=True)

    corr_next, potential = fields(corr, solute_pot, chi, site_charge)

    bricks = potential.astype(BF16).reshape(1, BRICK, 4, BRICK, 32, BRICK)
    bricks = bricks.transpose(0, 2, 4, 1, 3, 5).reshape(128, 512)
    answer = jnp.take(bricks, asked, axis=0, mode="clip")
    answer = lax.all_to_all(answer, "px", split_axis=0, concat_axis=0, tiled=True)
    sampled = jnp.take(answer, wanted, axis=0, mode="clip")
    weighted = (basis_values.astype(F32) * sampled.astype(F32)[:, :, None]).astype(BF16)
    embed = jnp.einsum("fcb,fcd->fbd", basis_values, weighted, preferred_element_type=F32)
    fock_out = fock_in.at[block_slot[0]].add(embed)
    return (corr_next, potential, fock_out)


def solution(mesh):
    return jax.shard_map(
        shards,
        mesh=mesh,
        in_specs=(
            P(None, "px", "py", None),
            P(None, "px", "py", None),
            P(None, None, None, "py", "px", None),
            P(),
            P(("px", "py"), None),
            P(("px", "py")),
            P(("px", "py"), None),
            P(("px", "py"), None, None),
            P(("px", "py"), None, None),
        ),
        out_specs=(P(None, "px", "py", None), P("px", "py", None), P(("px", "py"), None, None)),
        check_vma=False,
    )
```

time: 522 us -> 151 us (0.29)
  the two profiles are of different devices: /device:TPU:8 before, /device:TPU:1 now
where the time goes in v1:
time: 151 us; the launch traced here: 150 us
  Pallas kernels  84.8 us (56%)
  local copies, waits for them, and re-layouts  22.4 us (15%)
  starting transfers between devices  17.8 us (12%)
  waiting for transfers between devices  9.31 us (6%)
  matrix products  8.99 us (6%)
  other arithmetic  6.31 us (4%)
    pallas_call x1, Pallas kernels, fields(): pl.pallas_call(field_kernel, name='fields', out_shape=(jax.ShapeDtypeStru...  84.8 us
    all_to_all x1, starting transfers between devices, shards(): asked = lax.all_to_all(asked, 'px', split_axis=0, concat_axis=0, tiled=True)  12 us
    unnamed x30, local copies, waits for them, and re-layouts  9.39 us
    all_to_all x1, waiting for transfers between devices, shards(): lax.all_to_all(answer, 'px', split_axis=0, concat_axis=0, tiled=True)  9.31 us
    dot_general x1, matrix products, shards(): jnp.einsum('fcb,fcd->fbd', basis_values, weighted, preferred_element_type...  8.99 us
    all_to_all x1, starting transfers between devices, shards(): lax.all_to_all(answer, 'px', split_axis=0, concat_axis=0, tiled=True)  5.79 us
    scatter-add x1, other arithmetic, shards(): fock_out = fock_in.at[block_slot[0]].add(embed)  4.67 us
    dot_general x1, local copies, waits for them, and re-layouts, shards(): jnp.einsum('fcb,fcd->fbd', basis_values, weighted, preferred_element_type...  3.08 us
  transfers between devices with their start and end apart: 2, of which 1 were waited for; matrix products, arithmetic and copies ran while one was open for 4% of the time, Pallas kernels for 56%

profile of v1, /device:TPU:1, one launch (start us, length us, event | category | flops | bytes accessed | tf_op | source)
XLA Modules:
  0.0 150.4 jit_solution(11682232003732842165)
XLA Ops:
  0.6 0.0 copy-start.5
  0.7 0.8 copy-done.12
  1.5 0.2 convert_reduce_fusion
  1.7 0.8 scatter_custom_fusion
  2.5 0.7 all_to_all.14
  3.2 12.0 %all-to-all-start = ((s32[32,4,1]{1,2,0:T(1,128)}), s32[32,4,1]{1,2,0:T(1,128)}, u32[]{:S(2)}, u32[]{:S(2)}) async-start(s32[32,4,1]{1,2,0:T(1,128)} %bitcast.6), calls=%async_computation | async-start | bytes 32768 | tf_op jit(solution)/shard_map/all_to_all | solution.py:400
  15.2 1.1 copy-done.1
  16.4 1.0 copy-done.2
  17.4 1.0 copy-done.3
  18.4 1.0 copy-done.4
  19.4 0.9 copy-done.6
  20.3 0.9 copy-done.7
  21.2 0.9 copy-done.8
  22.1 84.8 %fields.1 = (f32[3,8,32,256]{3,2,1,0:T(8,128)S(1)}, f32[8,32,256]{2,1,0:T(8,128)S(1)}) custom-call(f32[3,8,32,256]{3,2,1,0:T(8,128)S(1)} %copy-done.1, bf16[3,8,32,256]{3,2,1,0:T(8,128)(2,1)S(1)} %copy-done.4, f32[3,3,2,16,8,256]{5,4,3,2,1,0:T(8,128)S(1)} %copy-done, f32[3]{0:T(128)S(1)} %copy-done.9, bf16[256,1024]{1,0:T(8,128)(2,1)S(1)} %copy-done.3, ...), custom_call_target="tpu_custom_call" | custom-call | tf_op jit(solution)/shard_map/fields/pallas_call | solution.py:361
  107.0 2.5 %reshape.51 = bf16[1,8,4,8,32,8]{5,4,3,2,1,0:T(8,128)(2,1)S(1)} reshape(bf16[8,32,256]{2,1,0:T(8,128)(2,1)S(1)} %convert_element_type.20) | data formatting | bytes 262144 | tf_op jit(solution)/shard_map/reshape | solution.py:404
  109.4 0.0 copy-start.13
  109.5 1.6 %copy.30 = bf16[1,4,32,8,8,8]{2,1,5,4,3,0:T(4,128)(2,1)} copy(bf16[1,4,32,8,8,8]{5,2,4,1,3,0:T(8,128)(2,1)S(1)} %bitcast.24) | data formatting | bytes 262144 | tf_op jit(solution)/shard_map/transpose | solution.py:405
  111.1 1.4 reshape.52
  112.5 0.1 copy.32
  112.6 0.5 broadcast.35
  113.1 1.4 reduce.3
  114.5 0.1 reshape.55
  114.6 0.8 gather_fusion
  115.5 0.7 all_to_all.16
  116.2 5.8 %all-to-all-start.1 = ((bf16[32,4,512]{2,1,0:T(4,128)(2,1)}), bf16[32,4,512]{2,1,0:T(4,128)(2,1)S(1)}, u32[]{:S(2)}, u32[]{:S(2)}) async-start(bf16[32,4,512]{2,1,0:T(4,128)(2,1)} %all_to_all.16), calls=%async_computation.1 | async-start | bytes 262144 | tf_op jit(solution)/shard_map/all_to_all | solution.py:407
  122.0 9.3 %all-to-all-done.1 = bf16[32,4,512]{2,1,0:T(4,128)(2,1)S(1)} async-done(((bf16[32,4,512]{2,1,0:T(4,128)(2,1)}), bf16[32,4,512]{2,1,0:T(4,128)(2,1)S(1)}, u32[]{:S(2)}, u32[]{:S(2)}) %all-to-all-start.1) | async-done | bytes 131104 | tf_op jit(solution)/shard_map/all_to_all | solution.py:407
  131.4 0.6 gather_fusion.1
  132.0 9.0 %fusion.2 = f32[32,128,128]{1,2,0:T(8,128)} fusion(bf16[32,512,128]{2,1,0:T(8,128)(2,1)} %param.22, f32[32,512]{1,0:T(8,128)S(1)} %convert_element_type.22), kind=kOutput, calls=%fused_computation.7 | convolution fusion | flops 543162368 | bytes 6356992 | tf_op jit(solution)/shard_map/fcb,fcd->fbd/dot_general | solution.py:410
  141.0 3.1 %copy.34 = f32[32,128,128]{2,1,0:T(8,128)} copy(f32[32,128,128]{1,2,0:T(8,128)} %fusion.2) | data formatting | bytes 4194304 | tf_op jit(solution)/shard_map/fcb,fcd->fbd/dot_general | solution.py:410
  144.1 4.7 %scatter_fusion = f32[32,128,128]{2,1,0:T(8,128)S(1)} fusion(f32[32,128,128]{2,1,0:T(8,128)S(1)} %copy-done.11, s32[32]{0:T(128)S(1)} %fusion.4, f32[32,128,128]{2,1,0:T(8,128)} %copy.34), kind=kCustom, calls=%fused_computation.3 | custom fusion | flops 524288 | bytes 6291584 | tf_op jit(solution)/shard_map/scatter-add | solution.py:411
  148.8 0.9 copy.41
  149.7 0.7 copy.42
  (26 shorter events, 0.1 us)
Async XLA Ops:
  0.6 14.6 %copy-start.5 = (bf16[256,256]{1,0:T(8,128)(2,1)S(1)}, bf16[256,256]{1,0:T(8,128)(2,1)}, u32[]{:S(2)}) copy-start(bf16[256,256]{1,0:T(8,128)(2,1)} %constant.27.clone.sl_ref) | copy-start | bytes 393220
  0.6 14.6 %copy-start = (f32[3,3,2,16,8,256]{5,4,3,2,1,0:T(8,128)S(1)}, f32[3,3,2,16,8,256]{5,4,3,2,1,0:T(8,128)}, u32[]{:S(2)}) copy-start(f32[3,3,2,16,8,256]{5,4,3,2,1,0:T(8,128)} %chi_ref.1) | copy-start | bytes 7077892
  0.7 14.6 %copy-start.9 = (f32[3]{0:T(128)S(1)}, f32[3]{0:T(128)}, u32[]{:S(2)}) copy-start(f32[3]{0:T(128)} %charge_ref.1) | copy-start | bytes 40
  0.7 0.8 copy-start.12
  3.2 109.4 %all-to-all-start = ((s32[32,4,1]{1,2,0:T(1,128)}), s32[32,4,1]{1,2,0:T(1,128)}, u32[]{:S(2)}, u32[]{:S(2)}) async-start(s32[32,4,1]{1,2,0:T(1,128)} %bitcast.6), calls=%async_computation | async-start | bytes 32768 | tf_op jit(solution)/shard_map/all_to_all | solution.py:400
  15.2 1.1 copy-start.1
  16.4 1.0 copy-start.2
  17.4 1.0 copy-start.3
  18.4 1.0 copy-start.4
  19.4 0.9 copy-start.6
  20.3 0.9 copy-start.7
  21.2 0.9 copy-start.8
  109.4 12.6 %copy-start.13 = (s32[1,32]{1,0:T(1,128)S(1)}, s32[1,32]{1,0:T(1,128)}, u32[]{:S(2)}) copy-start(s32[1,32]{1,0:T(1,128)} %param.21) | copy-start | bytes 388
  116.2 15.1 %all-to-all-start.1 = ((bf16[32,4,512]{2,1,0:T(4,128)(2,1)}), bf16[32,4,512]{2,1,0:T(4,128)(2,1)S(1)}, u32[]{:S(2)}, u32[]{:S(2)}) async-start(bf16[32,4,512]{2,1,0:T(4,128)(2,1)} %all_to_all.16), calls=%async_computation.1 | async-start | bytes 262144 | tf_op jit(solution)/shard_map/all_to_all | solution.py:407
  141.0 3.1 %copy-start.11 = (f32[32,128,128]{2,1,0:T(8,128)S(1)}, f32[32,128,128]{2,1,0:T(8,128)}, u32[]{:S(2)}) copy-start(f32[32,128,128]{2,1,0:T(8,128)} %param.23) | copy-start | bytes 6291460
  148.8 1.7 %copy-start.10 = (f32[32,128,128]{2,1,0:T(8,128)}, f32[32,128,128]{2,1,0:T(8,128)S(1)}, u32[]{:S(2)}) copy-start(f32[32,128,128]{2,1,0:T(8,128)S(1)} %scatter_fusion) | copy-start | bytes 6291460

commit v2 on v1

--- a/solution.py
+++ b/solution.py
@@ -18,7 +18,9 @@
 MESH = pl.DeviceIdType.MESH
 F32 = jnp.float32
 BF16 = jnp.bfloat16
-WIRE = jnp.float32
+WIRE = jnp.bfloat16
+FINE, STEEP, SLOPE = 11.0, 8.0, 3.0
+CENTRE_X, CENTRE_Z, CENTRE_Y, CENTRE_BACK = 5.0, 9.0, -5.0, -1.0
 
 
 def split(values):
@@ -45,12 +47,19 @@
     return np_split(spread) + np_split(cos) + np_split(sin)
 
 
-def encode(values):
-    return values.astype(WIRE)
-
-
-def decode(values):
-    return values.astype(F32)
+def encode(values, centre):
+    power = jnp.log2(jnp.abs(values)) - centre
+    power = SLOPE * power + (STEEP - SLOPE) * jnp.clip(power, -FINE, FINE)
+    coded = jnp.exp2(power)
+    return jnp.where(values < 0, -coded, coded).astype(WIRE)
+
+
+def decode(coded, centre):
+    coded = coded.astype(F32)
+    power = jnp.log2(jnp.abs(coded))
+    fine = jnp.clip(power, -FINE * STEEP, FINE * STEEP)
+    values = jnp.exp2(power * (1.0 / SLOPE) + fine * (1.0 / STEEP - 1.0 / SLOPE) + centre)
+    return jnp.where(coded < 0, -values, values)
 
 
 def dot(left, right):
@@ -116,7 +125,7 @@
         for pair in range(PY // 2):
             wide = dot3(dot, data, (xh_ref[:, 256 * pair:256 * pair + 256], xl_ref[:, 256 * pair:256 * pair + 256]))
             rows = jnp.where(lane_site == 0, wide[0:64], jnp.where(lane_site == 1, wide[64:128], wide[128:192]))
-            rows = encode(jnp.where(lane_site == 3, 0.0, rows))
+            rows = encode(jnp.where(lane_site == 3, 0.0, rows), CENTRE_X)
             s1[2 * pair, pl.ds(2 * yp, 2)] = rows[:, 0:128].reshape(2, 32, 128)
             s1[2 * pair + 1, pl.ds(2 * yp, 2)] = rows[:, 128:256].reshape(2, 32, 128)
 
@@ -152,7 +161,7 @@
     def z_forward(yp, carry):
         chunk = b1.at[pl.ds(2 * yp, 2)]
         pltpu.make_async_copy(chunk, chunk, recv1.at[yp]).wait()
-        data = split(jnp.concatenate([decode(b1[2 * yp]), decode(b1[2 * yp + 1])], axis=1))
+        data = split(jnp.concatenate([decode(b1[2 * yp + u], CENTRE_X) for u in range(2)], axis=1))
         cos_data = dot3(dot, cos, data)
         sin_data = dot3(dot, sin, data)
         halves = []
@@ -166,7 +175,7 @@
             packed_im = jnp.where(wave_edge, cd, jnp.where(wave_low, -sd_turn, -sd))
             packed = jnp.where(lane_re, packed_re, packed_im)
             halves.append(jnp.where(lane_spec, packed, usual).reshape(PX, 8, 128))
-        s2[:, yp] = encode(jnp.concatenate(halves, axis=1))
+        s2[:, yp] = encode(jnp.concatenate(halves, axis=1), CENTRE_Z)
         pltpu.make_async_copy(s2.at[px, yp], b2.at[px, yp], recv2.at[yp]).start()
 
         def send(step, inner):
@@ -182,21 +191,21 @@
 
     lax.fori_loop(0, 4, z_forward, 0)
 
-    def collect(buffer, sem):
+    def collect(buffer, sem, centre):
         def body(part, carry):
             chunk = buffer.at[:, part]
             pltpu.make_async_copy(chunk, chunk, sem.at[part]).wait()
 
             def place(source, inner):
                 start = pl.multiple_of(source * 64 + part * 16, 16)
-                ys[pl.ds(start, 16), :] = decode(buffer[source, part])
+                ys[pl.ds(start, 16), :] = decode(buffer[source, part], centre)
                 return inner
 
             return lax.fori_loop(0, PX, place, carry)
 
         lax.fori_loop(0, 4, body, 0)
 
-    collect(b2, recv2)
+    collect(b2, recv2, CENTRE_Z)
     chi_copy0.wait()
     chi_copy1.wait()
 
@@ -274,7 +283,8 @@
         turned = split(jnp.concatenate(turned, axis=0))
         back = dot3(dot_nt, cos, plain) + dot3(dot_nt, sin, turned)
         s3[:, kp] = encode(
-            jnp.concatenate([back[:, 128 * u:128 * u + 128].reshape(PX, 8, 128) for u in range(2)], axis=1)
+            jnp.concatenate([back[:, 128 * u:128 * u + 128].reshape(PX, 8, 128) for u in range(2)], axis=1),
+            CENTRE_Y,
         )
         pltpu.make_async_copy(s3.at[px, kp], b3.at[px, kp], recv3.at[kp]).start()
 
@@ -291,7 +301,7 @@
 
     lax.fori_loop(0, 4, y_both, 0)
 
-    collect(b3, recv3)
+    collect(b3, recv3, CENTRE_Y)
 
     def z_backward(yp, carry):
         plain, turned = [], []
@@ -308,7 +318,7 @@
             ))
         plain = split(jnp.concatenate(plain, axis=1))
         turned = split(jnp.concatenate(turned, axis=1))
-        back = encode(dot3(dot, cos, plain) + dot3(dot, sin, turned))
+        back = encode(dot3(dot, cos, plain) + dot3(dot, sin, turned), CENTRE_BACK)
         s4[2 * yp] = back[:, 0:128]
         s4[2 * yp + 1] = back[:, 128:256]
         pltpu.make_async_copy(
@@ -333,7 +343,7 @@
         chunk = b4.at[:, pl.ds(2 * yp, 2)]
         pltpu.make_async_copy(chunk, chunk, recv4.at[yp]).wait()
         rows = jnp.concatenate(
-            [decode(b4[j, pl.ds(2 * yp, 2)]).reshape(64, 128) for j in range(PY)], axis=1
+            [decode(b4[j, pl.ds(2 * yp, 2)], CENTRE_BACK).reshape(64, 128) for j in range(PY)], axis=1
         )
         field = jnp.concatenate([lane_field] * PY, axis=1)
         data = split(jnp.concatenate([jnp.where(field == f, rows, 0.0) for f in range(FIELDS)], axis=0))

time: 151 us -> 123 us (0.81)
  Pallas kernels: 84.8 us -> 57.6 us
    pallas_call x1, Pallas kernels: 84.8 us -> 57.6 us  [fields(): pl.pallas_call(field_kernel, name='fields', out_shape=(jax.ShapeDtypeStru...]
  transfers between devices with their start and end apart: 2 -> 2, of which waited for: 1 -> 1; matrix products, arithmetic and copies ran while one was open for 4% -> 5% of each run, Pallas kernels for 56% -> 47%
where the time goes in v2:
time: 123 us
  Pallas kernels  57.6 us (47%)
  local copies, waits for them, and re-layouts  22.4 us (18%)
  starting transfers between devices  17 us (14%)
  waiting for transfers between devices  9.43 us (8%)
  matrix products  8.99 us (7%)
  other arithmetic  6.31 us (5%)
    pallas_call x1, Pallas kernels, fields(): pl.pallas_call(field_kernel, name='fields', out_shape=(jax.ShapeDtypeStru...  57.6 us
    all_to_all x1, starting transfers between devices, shards(): asked = lax.all_to_all(asked, 'px', split_axis=0, concat_axis=0, tiled=True)  12 us
    all_to_all x1, waiting for transfers between devices, shards(): lax.all_to_all(answer, 'px', split_axis=0, concat_axis=0, tiled=True)  9.43 us
    unnamed x30, local copies, waits for them, and re-layouts  9.39 us
    dot_general x1, matrix products, shards(): jnp.einsum('fcb,fcd->fbd', basis_values, weighted, preferred_element_type...  8.99 us
    all_to_all x1, starting transfers between devices, shards(): lax.all_to_all(answer, 'px', split_axis=0, concat_axis=0, tiled=True)  5.05 us
    scatter-add x1, other arithmetic, shards(): fock_out = fock_in.at[block_slot[0]].add(embed)  4.67 us
    dot_general x1, local copies, waits for them, and re-layouts, shards(): jnp.einsum('fcb,fcd->fbd', basis_values, weighted, preferred_element_type...  3.08 us
  transfers between devices with their start and end apart: 2, of which 1 were waited for; matrix products, arithmetic and copies ran while one was open for 5% of the time, Pallas kernels for 47%

profile of v2, /device:TPU:1, one launch (start us, length us, event | category | flops | bytes accessed | tf_op | source)
XLA Modules:
  0.0 122.6 jit_solution(3795975774089458306)
XLA Ops:
  0.6 0.0 copy-start.5
  0.7 0.8 copy-done.12
  1.5 0.2 convert_reduce_fusion
  1.7 0.8 scatter_custom_fusion
  2.5 0.7 all_to_all.14
  3.2 12.0 %all-to-all-start = ((s32[32,4,1]{1,2,0:T(1,128)}), s32[32,4,1]{1,2,0:T(1,128)}, u32[]{:S(2)}, u32[]{:S(2)}) async-start(s32[32,4,1]{1,2,0:T(1,128)} %bitcast.6), calls=%async_computation | async-start | bytes 32768 | tf_op jit(solution)/shard_map/all_to_all | solution.py:410
  15.2 1.1 copy-done.1
  16.4 1.0 copy-done.2
  17.4 1.0 copy-done.3
  18.4 1.0 copy-done.4
  19.4 0.9 copy-done.6
  20.3 0.9 copy-done.7
  21.2 0.9 copy-done.8
  22.1 57.6 %fields.1 = (f32[3,8,32,256]{3,2,1,0:T(8,128)S(1)}, f32[8,32,256]{2,1,0:T(8,128)S(1)}) custom-call(f32[3,8,32,256]{3,2,1,0:T(8,128)S(1)} %copy-done.1, bf16[3,8,32,256]{3,2,1,0:T(8,128)(2,1)S(1)} %copy-done.4, f32[3,3,2,16,8,256]{5,4,3,2,1,0:T(8,128)S(1)} %copy-done, f32[3]{0:T(128)S(1)} %copy-done.9, bf16[256,1024]{1,0:T(8,128)(2,1)S(1)} %copy-done.3, ...), custom_call_target="tpu_custom_call" | custom-call | tf_op jit(solution)/shard_map/fields/pallas_call | solution.py:371
  79.8 2.5 %reshape.51 = bf16[1,8,4,8,32,8]{5,4,3,2,1,0:T(8,128)(2,1)S(1)} reshape(bf16[8,32,256]{2,1,0:T(8,128)(2,1)S(1)} %convert_element_type.20) | data formatting | bytes 262144 | tf_op jit(solution)/shard_map/reshape | solution.py:414
  82.3 0.0 copy-start.13
  82.3 1.6 %copy.30 = bf16[1,4,32,8,8,8]{2,1,5,4,3,0:T(4,128)(2,1)} copy(bf16[1,4,32,8,8,8]{5,2,4,1,3,0:T(8,128)(2,1)S(1)} %bitcast.24) | data formatting | bytes 262144 | tf_op jit(solution)/shard_map/transpose | solution.py:415
  83.9 1.4 %reshape.52 = bf16[128,512]{0,1:T(8,128)(2,1)S(1)} reshape(bf16[1,4,32,8,8,8]{2,1,5,4,3,0:T(4,128)(2,1)} %copy.30) | data formatting | bytes 262144 | tf_op jit(solution)/shard_map/reshape | solution.py:415
  85.3 0.1 copy.32
  85.4 0.5 broadcast.35
  85.9 1.4 %reduce.3 = s32[32,4]{1,0:T(8,128)S(1)} reduce(s32[32,4,1]{1,2,0:T(1,128)} %all-to-all-done, s32[]{:T(128)} %broadcast.35), dimensions={2}, to_apply=%all_to_all.15.reduce_sub_computation.3 | reduce | bytes 1028 | tf_op jit(solution)/shard_map/all_to_all | solution.py:410
  87.3 0.1 reshape.55
  87.5 0.8 gather_fusion
  88.3 0.7 all_to_all.16
  89.0 5.1 %all-to-all-start.1 = ((bf16[32,4,512]{2,1,0:T(4,128)(2,1)}), bf16[32,4,512]{2,1,0:T(4,128)(2,1)S(1)}, u32[]{:S(2)}, u32[]{:S(2)}) async-start(bf16[32,4,512]{2,1,0:T(4,128)(2,1)} %all_to_all.16), calls=%async_computation.1 | async-start | bytes 262144 | tf_op jit(solution)/shard_map/all_to_all | solution.py:417
  94.1 9.4 %all-to-all-done.1 = bf16[32,4,512]{2,1,0:T(4,128)(2,1)S(1)} async-done(((bf16[32,4,512]{2,1,0:T(4,128)(2,1)}), bf16[32,4,512]{2,1,0:T(4,128)(2,1)S(1)}, u32[]{:S(2)}, u32[]{:S(2)}) %all-to-all-start.1) | async-done | bytes 131104 | tf_op jit(solution)/shard_map/all_to_all | solution.py:417
  103.6 0.6 gather_fusion.1
  104.2 9.0 %fusion.2 = f32[32,128,128]{1,2,0:T(8,128)} fusion(bf16[32,512,128]{2,1,0:T(8,128)(2,1)} %param.22, f32[32,512]{1,0:T(8,128)S(1)} %convert_element_type.22), kind=kOutput, calls=%fused_computation.7 | convolution fusion | flops 543162368 | bytes 6356992 | tf_op jit(solution)/shard_map/fcb,fcd->fbd/dot_general | solution.py:420
  113.2 3.1 %copy.34 = f32[32,128,128]{2,1,0:T(8,128)} copy(f32[32,128,128]{1,2,0:T(8,128)} %fusion.2) | data formatting | bytes 4194304 | tf_op jit(solution)/shard_map/fcb,fcd->fbd/dot_general | solution.py:420
  116.3 4.7 %scatter_fusion = f32[32,128,128]{2,1,0:T(8,128)S(1)} fusion(f32[32,128,128]{2,1,0:T(8,128)S(1)} %copy-done.11, s32[32]{0:T(128)S(1)} %fusion.4, f32[32,128,128]{2,1,0:T(8,128)} %copy.34), kind=kCustom, calls=%fused_computation.3 | custom fusion | flops 524288 | bytes 6291584 | tf_op jit(solution)/shard_map/scatter-add | solution.py:421
  121.0 0.9 copy.41
  121.9 0.7 copy.42
  (26 shorter events, 0.1 us)
Async XLA Ops:
  0.6 14.6 %copy-start.5 = (bf16[256,256]{1,0:T(8,128)(2,1)S(1)}, bf16[256,256]{1,0:T(8,128)(2,1)}, u32[]{:S(2)}) copy-start(bf16[256,256]{1,0:T(8,128)(2,1)} %constant.27.clone.sl_ref) | copy-start | bytes 393220
  0.6 14.6 %copy-start = (f32[3,3,2,16,8,256]{5,4,3,2,1,0:T(8,128)S(1)}, f32[3,3,2,16,8,256]{5,4,3,2,1,0:T(8,128)}, u32[]{:S(2)}) copy-start(f32[3,3,2,16,8,256]{5,4,3,2,1,0:T(8,128)} %chi_ref.1) | copy-start | bytes 7077892
  0.7 14.6 %copy-start.9 = (f32[3]{0:T(128)S(1)}, f32[3]{0:T(128)}, u32[]{:S(2)}) copy-start(f32[3]{0:T(128)} %charge_ref.1) | copy-start | bytes 40
  0.7 0.8 copy-start.12
  3.2 82.2 %all-to-all-start = ((s32[32,4,1]{1,2,0:T(1,128)}), s32[32,4,1]{1,2,0:T(1,128)}, u32[]{:S(2)}, u32[]{:S(2)}) async-start(s32[32,4,1]{1,2,0:T(1,128)} %bitcast.6), calls=%async_computation | async-start | bytes 32768 | tf_op jit(solution)/shard_map/all_to_all | solution.py:410
  15.2 1.1 copy-start.1
  16.4 1.0 copy-start.2
  17.4 1.0 copy-start.3
  18.4 1.0 copy-start.4
  19.4 0.9 copy-start.6
  20.3 0.9 copy-start.7
  21.2 0.9 copy-start.8
  82.3 11.8 %copy-start.13 = (s32[1,32]{1,0:T(1,128)S(1)}, s32[1,32]{1,0:T(1,128)}, u32[]{:S(2)}) copy-start(s32[1,32]{1,0:T(1,128)} %param.21) | copy-start | bytes 388
  89.0 14.5 %all-to-all-start.1 = ((bf16[32,4,512]{2,1,0:T(4,128)(2,1)}), bf16[32,4,512]{2,1,0:T(4,128)(2,1)S(1)}, u32[]{:S(2)}, u32[]{:S(2)}) async-start(bf16[32,4,512]{2,1,0:T(4,128)(2,1)} %all_to_all.16), calls=%async_computation.1 | async-start | bytes 262144 | tf_op jit(solution)/shard_map/all_to_all | solution.py:417
  113.2 3.1 %copy-start.11 = (f32[32,128,128]{2,1,0:T(8,128)S(1)}, f32[32,128,128]{2,1,0:T(8,128)}, u32[]{:S(2)}) copy-start(f32[32,128,128]{2,1,0:T(8,128)} %param.23) | copy-start | bytes 6291460
  121.0 1.7 %copy-start.10 = (f32[32,128,128]{2,1,0:T(8,128)}, f32[32,128,128]{2,1,0:T(8,128)S(1)}, u32[]{:S(2)}) copy-start(f32[32,128,128]{2,1,0:T(8,128)S(1)} %scatter_fusion) | copy-start | bytes 6291460

commit v3 on v2

--- a/solution.py
+++ b/solution.py
@@ -85,10 +85,14 @@
 
 
 def field_kernel(
-    corr_ref, pot_ref, chi_ref, charge_ref, xh_ref, xl_ref, ch_ref, cl_ref, sh_ref, sl_ref,
-    corr_out, potential_out,
-    chi0, chi1, s1, b1, s2, b2, ys, s3, b3, s4, b4,
-    chi_sem, send1, recv1, send2, recv2, send3, recv3, send4, recv4,
+    charge_ref, corr_hbm, solute_hbm, chi_hbm, home_hbm, brick_hbm, slot_hbm, basis_hbm, fock_hbm,
+    xh_hbm, xl_hbm, ch_hbm, cl_hbm, sh_hbm, sl_hbm,
+    corr_out, potential_out, fock_out,
+    corr_ref, solute_ref, chi0, chi1, home_ref, brick_ref, slot_ref, basis_ref, fock_ref,
+    xh_ref, xl_ref, ch_ref, cl_ref, sh_ref, sl_ref,
+    s1, b1, s2, b2, ys, s3, b3, s4, b4,
+    ask_out, ask_in, ask_smem, info, info_smem, pot_ref, shuffled, brick_out, brick_in, turned_basis, tiles, samples,
+    in_sem, send1, recv1, send2, recv2, send3, recv3, send4, recv4, brick_sem,
 ):
     px = lax.axis_index("px")
     py = lax.axis_index("py")
@@ -102,12 +106,22 @@
         pl.semaphore_signal(barrier, inc=1, device_id=(px, lax.rem(py + step, PY)), device_id_type=MESH)
         return carry
 
+    pairs = (
+        (corr_hbm, corr_ref), (solute_hbm, solute_ref), (xh_hbm, xh_ref), (xl_hbm, xl_ref),
+        (ch_hbm, ch_ref), (cl_hbm, cl_ref), (sh_hbm, sh_ref), (sl_hbm, sl_ref),
+        (home_hbm, home_ref), (brick_hbm, brick_ref), (slot_hbm, slot_ref),
+        (chi_hbm.at[:, :, 0], chi0), (chi_hbm.at[:, :, 1, 0], chi1),
+        (basis_hbm, basis_ref), (fock_hbm, fock_ref),
+    )
+    loads = [pltpu.make_async_copy(source, to, in_sem.at[i]) for i, (source, to) in enumerate(pairs)]
+    for load in loads[:11]:
+        load.start()
     lax.fori_loop(1, PX, greet_px, 0)
     lax.fori_loop(1, PY, greet_py, 0)
-    chi_copy0 = pltpu.make_async_copy(chi_ref.at[:, :, 0], chi0, chi_sem.at[0])
-    chi_copy1 = pltpu.make_async_copy(chi_ref.at[:, :, 1, 0], chi1, chi_sem.at[1])
-    chi_copy0.start()
-    chi_copy1.start()
+    for load in loads[11:]:
+        load.start()
+    for load in loads[:4]:
+        load.wait()
 
     lane = lax.broadcasted_iota(jnp.int32, (1, 128), 1)
     lane_re = lane < 64
@@ -119,7 +133,7 @@
     def x_forward(yp, carry):
         parts = []
         for site in range(SITES):
-            rows = closure(corr_ref[site, pl.ds(2 * yp, 2)], pot_ref[site, pl.ds(2 * yp, 2)])
+            rows = closure(corr_ref[site, pl.ds(2 * yp, 2)], solute_ref[site, pl.ds(2 * yp, 2)])
             parts.append(rows.reshape(64, N))
         data = split(jnp.concatenate(parts, axis=0))
         for pair in range(PY // 2):
@@ -151,6 +165,44 @@
 
     lax.fori_loop(0, 4, x_forward, 0)
 
+    for load in loads[8:11]:
+        load.wait()
+    home = home_ref[...]
+    brick = brick_ref[...]
+    down = lax.broadcasted_iota(jnp.int32, (32, 32), 0)
+    across = lax.broadcasted_iota(jnp.int32, (32, 32), 1)
+    home_down = jnp.sum(jnp.where(down == across, home, 0), axis=1, keepdims=True)
+    place = jnp.sum(jnp.where((home_down == home) & (down < across), 1, 0), axis=0, keepdims=True)
+    wide_lane = lax.broadcasted_iota(jnp.int32, (32, 128), 1)
+    asked = jnp.zeros((32, 128), jnp.int32)
+    for k in range(MOST):
+        found = jnp.sum(jnp.where((home == down) & (place == k), brick, 0), axis=1, keepdims=True)
+        asked = jnp.where(wide_lane == k, jnp.clip(found, 0, 127), asked)
+    for other in range(PX):
+        ask_out[other] = asked[other:other + 1]
+    table = jnp.zeros((32, 128), jnp.int32)
+    for k, (value, most) in enumerate(((across, 31), (home, PX - 1), (place, MOST - 1))):
+        found = jnp.sum(jnp.where(slot_ref[...] == down, value, 0), axis=1, keepdims=True)
+        table = jnp.where(wide_lane == k, jnp.clip(found, 0, most), table)
+    info[...] = table
+    info_copy = pltpu.make_async_copy(info, info_smem, brick_sem.at[0])
+    info_copy.start()
+    pltpu.make_async_copy(ask_out.at[px], ask_in.at[px], brick_sem.at[2]).start()
+
+    def ask(step, carry):
+        other = lax.rem(px + step, PX)
+        pltpu.make_async_remote_copy(
+            src_ref=ask_out.at[other], dst_ref=ask_in.at[px],
+            send_sem=brick_sem.at[1], recv_sem=brick_sem.at[2],
+            device_id=(other, py), device_id_type=MESH,
+        ).start()
+        return carry
+
+    lax.fori_loop(1, PX, ask, 0)
+    for load in loads[4:8]:
+        load.wait()
+    loads[13].wait()
+
     cos = (ch_ref[...], cl_ref[...])
     sin = (sh_ref[...], sl_ref[...])
     wave = lax.broadcasted_iota(jnp.int32, (N, 1), 0)
@@ -159,6 +211,11 @@
     wave_high = wave > N // 2
 
     def z_forward(yp, carry):
+        def turn_basis(item, inner):
+            turned_basis[8 * yp + item] = basis_ref[8 * yp + item].T
+            return inner
+
+        lax.fori_loop(0, 8, turn_basis, 0)
         chunk = b1.at[pl.ds(2 * yp, 2)]
         pltpu.make_async_copy(chunk, chunk, recv1.at[yp]).wait()
         data = split(jnp.concatenate([decode(b1[2 * yp + u], CENTRE_X) for u in range(2)], axis=1))
@@ -206,8 +263,8 @@
         lax.fori_loop(0, 4, body, 0)
 
     collect(b2, recv2, CENTRE_Z)
-    chi_copy0.wait()
-    chi_copy1.wait()
+    loads[11].wait()
+    loads[12].wait()
 
     row = lax.broadcasted_iota(jnp.int32, (R, 1), 0)
     first = (row == 0) & (py == 0)
@@ -350,10 +407,91 @@
         back = dot3(dot_nt, data, (xh_ref[...], xl_ref[...]))
         for f in range(SITES):
             corr_out[f, pl.ds(2 * yp, 2)] = back[64 * f:64 * f + 64].reshape(2, 32, N)
-        potential_out[pl.ds(2 * yp, 2)] = back[192:256].reshape(2, 32, N)
+        potential = back[192:256].reshape(2, 32, N)
+        potential_out[pl.ds(2 * yp, 2)] = potential
+        pot_ref[0, pl.ds(2 * yp, 2)] = potential[:, :, 0:128]
+        pot_ref[1, pl.ds(2 * yp, 2)] = potential[:, :, 128:256]
         return carry
 
     lax.fori_loop(0, 4, x_backward, 0)
+
+    pltpu.make_async_copy(ask_in, ask_in, brick_sem.at[2]).wait()
+    ask_copy = pltpu.make_async_copy(ask_in, ask_smem, brick_sem.at[3])
+    ask_copy.start()
+    lane_row = lane // 32
+
+    def shuffle(bz, carry):
+        for half in range(2):
+            slabs = [pot_ref[half, y, pl.ds(8 * bz, 8), :] for y in range(8)]
+            for quad in range(4):
+                rows = []
+                for u in range(2):
+                    row = slabs[u]
+                    if quad:
+                        row = pltpu.roll(row, 128 - 32 * quad, 1)
+                    for yg in range(1, 4):
+                        move = 32 * ((yg - quad) % 4)
+                        other = slabs[2 * yg + u]
+                        other = pltpu.roll(other, move, 1) if move else other
+                        row = jnp.where(lane_row == yg, other, row)
+                    rows.append(row)
+                shuffled[8 * bz + 4 * half + quad] = jnp.concatenate(rows, axis=0)
+        return carry
+
+    lax.fori_loop(0, 4, shuffle, 0)
+    ask_copy.wait()
+    lane_place = lax.rem(lane // BRICK, MOST)
+
+    def answer(step, carry):
+        other = lax.rem(px + step, PX)
+        tile = jnp.zeros((16, 128), F32)
+        for k in range(MOST):
+            index = ask_smem[other, 0, k]
+            moved = pltpu.roll(shuffled[index // 4], lax.rem(BRICK * (k - lax.rem(index, 4)) + 128, 128), 1)
+            tile = jnp.where(lane_place == k, moved, tile)
+        brick_out[other] = tile.astype(BF16)
+
+        @pl.when(step > 0)
+        def _():
+            pltpu.make_async_remote_copy(
+                src_ref=brick_out.at[other], dst_ref=brick_in.at[px],
+                send_sem=brick_sem.at[4], recv_sem=brick_sem.at[5],
+                device_id=(other, py), device_id_type=MESH,
+            ).start()
+
+        return carry
+
+    lax.fori_loop(0, PX, answer, 0)
+    pltpu.make_async_copy(brick_out.at[px], brick_in.at[px], brick_sem.at[5]).start()
+    info_copy.wait()
+    loads[14].wait()
+    pltpu.make_async_copy(brick_in, brick_in, brick_sem.at[5]).wait()
+
+    def take(slot, carry):
+        tile = brick_in[info_smem[slot, 1]].astype(F32)
+        tile = pltpu.roll(tile, lax.rem(128 - BRICK * info_smem[slot, 2], 128), 1)
+        tiles[pl.ds(pl.multiple_of(16 * slot, 16), 16), :] = tile.astype(BF16)
+        return carry
+
+    lax.fori_loop(0, 32, take, 0)
+    cell = lax.broadcasted_iota(jnp.int32, (128, 512), 1)
+    origin = lax.broadcasted_iota(jnp.int32, (128, 512), 0)
+    spread = (origin == 32 * (cell // 128) + lax.rem(cell, BRICK)).astype(F32).astype(BF16)
+    wide = dot(tiles[...], spread)
+    tile_row = lax.broadcasted_iota(jnp.int32, (512, 512), 0)
+    tile_cell = lax.broadcasted_iota(jnp.int32, (512, 512), 1)
+    wide = jnp.where(lax.rem(tile_row, 16) == lax.rem(tile_cell, 128) // BRICK, wide, 0.0).astype(BF16)
+    slot_down = lax.broadcasted_iota(jnp.int32, (32, 512), 0)
+    slot_cell = lax.broadcasted_iota(jnp.int32, (32, 512), 1)
+    samples[...] = dot((slot_down == slot_cell // 16).astype(F32).astype(BF16), wide)
+
+    def embed(slot, carry):
+        basis = turned_basis[info_smem[slot, 0]]
+        weighted = basis * samples[pl.ds(slot, 1), :].astype(BF16)
+        fock_out[slot] = fock_ref[slot] + dot_nt(basis, weighted)
+        return carry
+
+    lax.fori_loop(0, 32, embed, 0)
 
     for part in range(4):
         sent = s1.at[pl.ds(0, PY - 1), pl.ds(0, 2)]
@@ -363,23 +501,45 @@
         pltpu.make_async_copy(sent, sent, send3.at[part]).wait()
         sent = s4.at[pl.ds(0, 2), pl.ds(0, 32 * (PY - 1))]
         pltpu.make_async_copy(sent, sent, send4.at[part]).wait()
-
-
-def fields(corr, solute_pot, chi, site_charge):
+    sent = ask_out.at[pl.ds(0, PX - 1)]
+    pltpu.make_async_copy(sent, sent, brick_sem.at[1]).wait()
+    sent = brick_out.at[pl.ds(0, PX - 1)]
+    pltpu.make_async_copy(sent, sent, brick_sem.at[4]).wait()
+
+
+def shards(
+    corr, solute_pot, chi, site_charge, home_slab, brick_index, block_slot, basis_values, fock_in
+):
     vmem = pl.BlockSpec(memory_space=pltpu.VMEM)
+    hbm = pl.BlockSpec(memory_space=pltpu.HBM)
     dma = pltpu.SemaphoreType.DMA((4,))
+    frags = home_slab.shape[0]
     return pl.pallas_call(
         field_kernel,
         name="fields",
         out_shape=(
             jax.ShapeDtypeStruct((SITES, 8, 32, N), F32),
             jax.ShapeDtypeStruct((8, 32, N), F32),
+            jax.ShapeDtypeStruct(fock_in.shape, F32),
         ),
-        in_specs=[vmem, vmem, pl.BlockSpec(memory_space=pl.ANY), pl.BlockSpec(memory_space=pltpu.SMEM)] + [vmem] * 6,
-        out_specs=(vmem, vmem),
+        in_specs=[pl.BlockSpec(memory_space=pltpu.SMEM)] + [hbm] * 14,
+        out_specs=(vmem,) * 3,
         scratch_shapes=[
+            pltpu.VMEM(corr.shape, F32),
+            pltpu.VMEM(solute_pot.shape, BF16),
             pltpu.VMEM((SITES, SITES, R, 8, N), F32),
             pltpu.VMEM((SITES, SITES, 8, N), F32),
+            pltpu.VMEM((1, frags), jnp.int32),
+            pltpu.VMEM((1, frags), jnp.int32),
+            pltpu.VMEM((1, frags), jnp.int32),
+            pltpu.VMEM(basis_values.shape, BF16),
+            pltpu.VMEM(fock_in.shape, F32),
+            pltpu.VMEM((N, PY * 128), BF16),
+            pltpu.VMEM((N, PY * 128), BF16),
+            pltpu.VMEM((N, N), BF16),
+            pltpu.VMEM((N, N), BF16),
+            pltpu.VMEM((N, N), BF16),
+            pltpu.VMEM((N, N), BF16),
             pltpu.VMEM((PY, 8, 32, 128), WIRE),
             pltpu.VMEM((8, N, 128), WIRE),
             pltpu.VMEM((PX, 4, 16, 128), WIRE),
@@ -389,37 +549,27 @@
             pltpu.VMEM((PX, 4, 16, 128), WIRE),
             pltpu.VMEM((8, N, 128), WIRE),
             pltpu.VMEM((PY, 8, 32, 128), WIRE),
-            pltpu.SemaphoreType.DMA((2,)),
-        ] + [dma] * 8,
+            pltpu.VMEM((PX, 1, 128), jnp.int32),
+            pltpu.VMEM((PX, 1, 128), jnp.int32),
+            pltpu.SMEM((PX, 1, 128), jnp.int32),
+            pltpu.VMEM((frags, 128), jnp.int32),
+            pltpu.SMEM((frags, 128), jnp.int32),
+            pltpu.VMEM((2, 8, 32, 128), F32),
+            pltpu.VMEM((32, 16, 128), F32),
+            pltpu.VMEM((PX, 16, 128), BF16),
+            pltpu.VMEM((PX, 16, 128), BF16),
+            pltpu.VMEM((frags, 128, 512), BF16),
+            pltpu.VMEM((frags * 16, 128), BF16),
+            pltpu.VMEM((frags, 512), F32),
+            pltpu.SemaphoreType.DMA((15,)),
+        ] + [dma] * 8 + [pltpu.SemaphoreType.DMA((6,))],
         compiler_params=pltpu.CompilerParams(
-            collective_id=0, has_side_effects=True, vmem_limit_bytes=40 * 2**20
+            collective_id=0, has_side_effects=True, vmem_limit_bytes=48 * 2**20
         ),
-    )(corr, solute_pot, chi, site_charge, *[jnp.asarray(table) for table in tables()])
-
-
-def shards(
-    corr, solute_pot, chi, site_charge, home_slab, brick_index, block_slot, basis_values, fock_in
-):
-    home = home_slab[:, 0]
-    frags = home.shape[0]
-    same = home[:, None] == home[None, :]
-    earlier = jnp.arange(frags)[None, :] < jnp.arange(frags)[:, None]
-    place = jnp.sum((same & earlier).astype(jnp.int32), axis=1)
-    wanted = home * MOST + place
-    asked = jnp.zeros((PX * MOST,), jnp.int32).at[wanted].set(brick_index)
-    asked = lax.all_to_all(asked, "px", split_axis=0, concat_axis=0, tiled=True)
-
-    corr_next, potential = fields(corr, solute_pot, chi, site_charge)
-
-    bricks = potential.astype(BF16).reshape(1, BRICK, 4, BRICK, 32, BRICK)
-    bricks = bricks.transpose(0, 2, 4, 1, 3, 5).reshape(128, 512)
-    answer = jnp.take(bricks, asked, axis=0, mode="clip")
-    answer = lax.all_to_all(answer, "px", split_axis=0, concat_axis=0, tiled=True)
-    sampled = jnp.take(answer, wanted, axis=0, mode="clip")
-    weighted = (basis_values.astype(F32) * sampled.astype(F32)[:, :, None]).astype(BF16)
-    embed = jnp.einsum("fcb,fcd->fbd", basis_values, weighted, preferred_element_type=F32)
-    fock_out = fock_in.at[block_slot[0]].add(embed)
-    return (corr_next, potential, fock_out)
+    )(
+        site_charge, corr, solute_pot, chi, home_slab.reshape(1, frags), brick_index.reshape(1, frags),
+        block_slot, basis_values, fock_in, *[jnp.asarray(table) for table in tables()],
+    )
 
 
 def solution(mesh):

time: 123 us -> 91.3 us (0.74)
  Pallas kernels: 57.6 us -> 76.9 us
  starting transfers between devices: 17 us -> 0 us
  waiting for transfers between devices: 9.43 us -> 0 us
  local copies, waits for them, and re-layouts: 22.4 us -> 13.3 us
  matrix products: 8.99 us -> 0 us
  other arithmetic: 6.31 us -> 0 us
    pallas_call x1, Pallas kernels: 57.6 us -> 76.9 us  [shards(): pl.pallas_call(field_kernel, name='fields', out_shape=(jax.ShapeDtypeStru...]
    all_to_all x2 -> x0, starting transfers between devices: 17 us -> none  [the longest x1 12 us: shards(): asked = lax.all_to_all(asked, 'px', split_axis=0, concat_axis=0, tiled=True)]
    all_to_all x2 -> x0, waiting for transfers between devices: 9.43 us -> none  [the longest x1 9.43 us: shards(): lax.all_to_all(answer, 'px', split_axis=0, concat_axis=0, tiled=True)]
    dot_general x1 -> x0, matrix products: 8.99 us -> none  [shards(): jnp.einsum('fcb,fcd->fbd', basis_values, weighted, preferred_element_type...]
    scatter-add x1 -> x0, other arithmetic: 4.67 us -> none  [shards(): fock_out = fock_in.at[block_slot[0]].add(embed)]
    reshape x3 -> x0, local copies, waits for them, and re-layouts: 3.97 us -> none  [the longest x1 2.47 us: shards(): bricks = potential.astype(BF16).reshape(1, BRICK, 4, BRICK, 32, BRICK)]
    unnamed x30 -> x27, local copies, waits for them, and re-layouts: 9.39 us -> 13.3 us
    dot_general x1 -> x0, local copies, waits for them, and re-layouts: 3.08 us -> none  [shards(): jnp.einsum('fcb,fcd->fbd', basis_values, weighted, preferred_element_type...]
  transfers between devices with their start and end apart: 2 -> 0, of which waited for: 1 -> 0; matrix products, arithmetic and copies ran while one was open for 5% -> 0% of each run, Pallas kernels for 47% -> 0%
where the time goes in v3:
time: 91.3 us; the launch traced here: 90.9 us
  Pallas kernels  76.9 us (84%)
  local copies, waits for them, and re-layouts  13.3 us (15%)
    pallas_call x1, Pallas kernels, shards(): pl.pallas_call(field_kernel, name='fields', out_shape=(jax.ShapeDtypeStru...  76.9 us
    unnamed x27, local copies, waits for them, and re-layouts  13.3 us

profile of v3, /device:TPU:1, one launch (start us, length us, event | category | flops | bytes accessed | tf_op | source)
XLA Modules:
  0.0 90.9 jit_solution(3521082067568369893)
XLA Ops:
  0.6 0.0 copy-start
  0.6 1.1 %copy-done = f32[3,8,32,256]{3,2,1,0:T(8,128)S(1)} copy-done((f32[3,8,32,256]{3,2,1,0:T(8,128)S(1)}, f32[3,8,32,256]{3,2,1,0:T(8,128)}, u32[]{:S(2)}) %copy-start) | copy-done | bytes 786456
  1.8 0.0 copy-start.1
  1.8 1.0 %copy-done.1 = bf16[256,1024]{1,0:T(8,128)(2,1)S(1)} copy-done((bf16[256,1024]{1,0:T(8,128)(2,1)S(1)}, bf16[256,1024]{1,0:T(8,128)(2,1)}, u32[]{:S(2)}) %copy-start.1) | copy-done | bytes 524312
  2.8 0.0 copy-start.2
  2.8 1.0 %copy-done.2 = bf16[256,1024]{1,0:T(8,128)(2,1)S(1)} copy-done((bf16[256,1024]{1,0:T(8,128)(2,1)S(1)}, bf16[256,1024]{1,0:T(8,128)(2,1)}, u32[]{:S(2)}) %copy-start.2) | copy-done | bytes 524312
  3.9 0.0 copy-start.3
  3.9 1.0 %copy-done.3 = bf16[3,8,32,256]{3,2,1,0:T(8,128)(2,1)S(1)} copy-done((bf16[3,8,32,256]{3,2,1,0:T(8,128)(2,1)S(1)}, bf16[3,8,32,256]{3,2,1,0:T(8,128)(2,1)}, u32[]{:S(2)}) %copy-start.3) | copy-done | bytes 393240
  4.8 0.0 copy-start.4
  4.9 0.9 copy-done.4
  5.8 0.0 copy-start.5
  5.8 0.9 copy-done.5
  6.7 0.0 copy-start.6
  6.7 0.9 copy-done.6
  7.6 0.0 copy-start.7
  7.6 0.9 copy-done.7
  8.5 0.0 copy-start.8
  8.5 0.7 copy-done.8
  9.1 0.0 copy-start.9
  9.1 0.7 copy-done.9
  9.8 0.0 copy-start.10
  9.8 0.7 copy-done.10
  10.4 0.0 copy-start.11
  10.4 0.7 copy-done.11
  11.1 76.9 %fields.1 = (f32[3,8,32,256]{3,2,1,0:T(8,128)S(1)}, f32[8,32,256]{2,1,0:T(8,128)S(1)}, f32[32,128,128]{2,1,0:T(8,128)S(1)}) custom-call(f32[3]{0:T(128)S(1)} %copy-done.8, f32[3,8,32,256]{3,2,1,0:T(8,128)S(1)} %copy-done, bf16[3,8,32,256]{3,2,1,0:T(8,128)(2,1)S(1)} %copy-done.3, f32[3,3,2,16,8,256]{5,4,3,2,1,0:T(8,128)} %chi_hbm.1, s32[1,32]{1,0:T(1,128)S(1)} %bitcast.2, ...), custom_call_target="tpu_custom_call" | custom-call | tf_op jit(solution)/shard_map/fields/pallas_call | solution.py:517
  88.0 0.9 copy.21
  88.9 0.7 copy.22
  89.6 1.3 %copy.23 = f32[32,128,128]{2,1,0:T(8,128)} copy(f32[32,128,128]{2,1,0:T(8,128)S(1)} %get-tuple-element.8) | data formatting | bytes 4194304
Async XLA Ops:
  0.6 1.1 %copy-start = (f32[3,8,32,256]{3,2,1,0:T(8,128)S(1)}, f32[3,8,32,256]{3,2,1,0:T(8,128)}, u32[]{:S(2)}) copy-start(f32[3,8,32,256]{3,2,1,0:T(8,128)} %corr_hbm.1) | copy-start | bytes 2359300
  1.8 1.0 %copy-start.1 = (bf16[256,1024]{1,0:T(8,128)(2,1)S(1)}, bf16[256,1024]{1,0:T(8,128)(2,1)}, u32[]{:S(2)}) copy-start(bf16[256,1024]{1,0:T(8,128)(2,1)} %constant.13.clone.xl_hbm) | copy-start | bytes 1572868
  2.8 1.0 %copy-start.2 = (bf16[256,1024]{1,0:T(8,128)(2,1)S(1)}, bf16[256,1024]{1,0:T(8,128)(2,1)}, u32[]{:S(2)}) copy-start(bf16[256,1024]{1,0:T(8,128)(2,1)} %constant.12.clone.xh_hbm) | copy-start | bytes 1572868
  3.9 1.0 %copy-start.3 = (bf16[3,8,32,256]{3,2,1,0:T(8,128)(2,1)S(1)}, bf16[3,8,32,256]{3,2,1,0:T(8,128)(2,1)}, u32[]{:S(2)}) copy-start(bf16[3,8,32,256]{3,2,1,0:T(8,128)(2,1)} %solute_hbm.1) | copy-start | bytes 1179652
  4.8 0.9 copy-start.4
  5.8 0.9 copy-start.5
  6.7 0.9 copy-start.6
  7.6 0.9 copy-start.7
  8.5 0.7 copy-start.8
  9.1 0.7 copy-start.9
  9.8 0.7 copy-start.10
  10.4 0.7 copy-start.11

commit v4 on v3

--- a/solution.py
+++ b/solution.py
@@ -87,12 +87,13 @@
 def field_kernel(
     charge_ref, corr_hbm, solute_hbm, chi_hbm, home_hbm, brick_hbm, slot_hbm, basis_hbm, fock_hbm,
     xh_hbm, xl_hbm, ch_hbm, cl_hbm, sh_hbm, sl_hbm,
+    corr_hbm_out, potential_hbm_out, fock_hbm_out,
     corr_out, potential_out, fock_out,
     corr_ref, solute_ref, chi0, chi1, home_ref, brick_ref, slot_ref, basis_ref, fock_ref,
     xh_ref, xl_ref, ch_ref, cl_ref, sh_ref, sl_ref,
     s1, b1, s2, b2, ys, s3, b3, s4, b4,
     ask_out, ask_in, ask_smem, info, info_smem, pot_ref, shuffled, brick_out, brick_in, turned_basis, tiles, samples,
-    in_sem, send1, recv1, send2, recv2, send3, recv3, send4, recv4, brick_sem,
+    in_sem, send1, recv1, send2, recv2, send3, recv3, send4, recv4, brick_sem, corr_sem, potential_sem, fock_sem,
 ):
     px = lax.axis_index("px")
     py = lax.axis_index("py")
@@ -201,7 +202,6 @@
     lax.fori_loop(1, PX, ask, 0)
     for load in loads[4:8]:
         load.wait()
-    loads[13].wait()
 
     cos = (ch_ref[...], cl_ref[...])
     sin = (sh_ref[...], sl_ref[...])
@@ -211,11 +211,6 @@
     wave_high = wave > N // 2
 
     def z_forward(yp, carry):
-        def turn_basis(item, inner):
-            turned_basis[8 * yp + item] = basis_ref[8 * yp + item].T
-            return inner
-
-        lax.fori_loop(0, 8, turn_basis, 0)
         chunk = b1.at[pl.ds(2 * yp, 2)]
         pltpu.make_async_copy(chunk, chunk, recv1.at[yp]).wait()
         data = split(jnp.concatenate([decode(b1[2 * yp + u], CENTRE_X) for u in range(2)], axis=1))
@@ -253,15 +248,23 @@
             chunk = buffer.at[:, part]
             pltpu.make_async_copy(chunk, chunk, sem.at[part]).wait()
 
-            def place(source, inner):
-                start = pl.multiple_of(source * 64 + part * 16, 16)
-                ys[pl.ds(start, 16), :] = decode(buffer[source, part], centre)
+            def place(group, inner):
+                sources = pl.ds(8 * group, 8)
+                ys[sources, pl.ds(pl.multiple_of(16 * part, 16), 16), :] = decode(buffer[sources, part], centre)
                 return inner
 
-            return lax.fori_loop(0, PX, place, carry)
+            return lax.fori_loop(0, PX // 8, place, carry)
 
         lax.fori_loop(0, 4, body, 0)
 
+    pencils = ys.reshape(PX * 64, 128)
+
+    def turn_basis(item, carry):
+        turned_basis[item] = basis_ref[item].T
+        return carry
+
+    loads[13].wait()
+    lax.fori_loop(0, 32, turn_basis, 0)
     collect(b2, recv2, CENTRE_Z)
     loads[11].wait()
     loads[12].wait()
@@ -298,7 +301,7 @@
     def y_both(kp, carry):
         plain, turned = [], []
         rows = jnp.concatenate(
-            [ys[pl.ds(2 * kp + u, N, stride=8), :].T for u in range(2)], axis=0
+            [pencils[pl.ds(2 * kp + u, N, stride=8), :].T for u in range(2)], axis=0
         )
         data = split(rows)
         cos_data = dot3(dot, data, cos)
@@ -363,7 +366,7 @@
     def z_backward(yp, carry):
         plain, turned = [], []
         for u in range(2):
-            data = ys[pl.ds(2 * yp + u, N, stride=8), :]
+            data = pencils[pl.ds(2 * yp + u, N, stride=8), :]
             turn = pltpu.roll(data, 64, 1)
             packed_re = jnp.where(wave_edge, data, jnp.where(wave_low, data + data, 0.0))
             packed_im = jnp.where(wave_edge, data, jnp.where(wave_low, 0.0, turn + turn))
@@ -411,6 +414,9 @@
         potential_out[pl.ds(2 * yp, 2)] = potential
         pot_ref[0, pl.ds(2 * yp, 2)] = potential[:, :, 0:128]
         pot_ref[1, pl.ds(2 * yp, 2)] = potential[:, :, 128:256]
+        slabs = pl.ds(2 * yp, 2)
+        pltpu.make_async_copy(corr_out.at[:, slabs], corr_hbm_out.at[:, slabs], corr_sem.at[yp]).start()
+        pltpu.make_async_copy(potential_out.at[slabs], potential_hbm_out.at[slabs], potential_sem.at[yp]).start()
         return carry
 
     lax.fori_loop(0, 4, x_backward, 0)
@@ -461,7 +467,7 @@
 
         return carry
 
-    lax.fori_loop(0, PX, answer, 0)
+    lax.fori_loop(0, PX, answer, 0, unroll=2)
     pltpu.make_async_copy(brick_out.at[px], brick_in.at[px], brick_sem.at[5]).start()
     info_copy.wait()
     loads[14].wait()
@@ -473,7 +479,7 @@
         tiles[pl.ds(pl.multiple_of(16 * slot, 16), 16), :] = tile.astype(BF16)
         return carry
 
-    lax.fori_loop(0, 32, take, 0)
+    lax.fori_loop(0, 32, take, 0, unroll=4)
     cell = lax.broadcasted_iota(jnp.int32, (128, 512), 1)
     origin = lax.broadcasted_iota(jnp.int32, (128, 512), 0)
     spread = (origin == 32 * (cell // 128) + lax.rem(cell, BRICK)).astype(F32).astype(BF16)
@@ -485,13 +491,24 @@
     slot_cell = lax.broadcasted_iota(jnp.int32, (32, 512), 1)
     samples[...] = dot((slot_down == slot_cell // 16).astype(F32).astype(BF16), wide)
 
-    def embed(slot, carry):
-        basis = turned_basis[info_smem[slot, 0]]
-        weighted = basis * samples[pl.ds(slot, 1), :].astype(BF16)
-        fock_out[slot] = fock_ref[slot] + dot_nt(basis, weighted)
-        return carry
-
-    lax.fori_loop(0, 32, embed, 0)
+    def embed(group, carry):
+        for item in range(4):
+            slot = 4 * group + item
+            fragment = info_smem[slot, 0]
+            weighted = turned_basis[fragment] * samples[pl.ds(slot, 1), :].astype(BF16)
+            fock_out[slot] = fock_ref[slot] + dot(weighted, basis_ref[fragment])
+        slots = pl.ds(4 * group, 4)
+        pltpu.make_async_copy(fock_out.at[slots], fock_hbm_out.at[slots], fock_sem.at[group]).start()
+        return carry
+
+    lax.fori_loop(0, 8, embed, 0)
+    for part in range(4):
+        slabs = pl.ds(2 * part, 2)
+        pltpu.make_async_copy(corr_out.at[:, slabs], corr_hbm_out.at[:, slabs], corr_sem.at[part]).wait()
+        pltpu.make_async_copy(potential_out.at[slabs], potential_hbm_out.at[slabs], potential_sem.at[part]).wait()
+    for part in range(8):
+        slots = pl.ds(4 * part, 4)
+        pltpu.make_async_copy(fock_out.at[slots], fock_hbm_out.at[slots], fock_sem.at[part]).wait()
 
     for part in range(4):
         sent = s1.at[pl.ds(0, PY - 1), pl.ds(0, 2)]
@@ -510,7 +527,6 @@
 def shards(
     corr, solute_pot, chi, site_charge, home_slab, brick_index, block_slot, basis_values, fock_in
 ):
-    vmem = pl.BlockSpec(memory_space=pltpu.VMEM)
     hbm = pl.BlockSpec(memory_space=pltpu.HBM)
     dma = pltpu.SemaphoreType.DMA((4,))
     frags = home_slab.shape[0]
@@ -523,8 +539,11 @@
             jax.ShapeDtypeStruct(fock_in.shape, F32),
         ),
         in_specs=[pl.BlockSpec(memory_space=pltpu.SMEM)] + [hbm] * 14,
-        out_specs=(vmem,) * 3,
+        out_specs=(hbm,) * 3,
         scratch_shapes=[
+            pltpu.VMEM(corr.shape, F32),
+            pltpu.VMEM(corr.shape[1:], F32),
+            pltpu.VMEM(fock_in.shape, F32),
             pltpu.VMEM(corr.shape, F32),
             pltpu.VMEM(solute_pot.shape, BF16),
             pltpu.VMEM((SITES, SITES, R, 8, N), F32),
@@ -544,7 +563,7 @@
             pltpu.VMEM((8, N, 128), WIRE),
             pltpu.VMEM((PX, 4, 16, 128), WIRE),
             pltpu.VMEM((PX, 4, 16, 128), WIRE),
-            pltpu.VMEM((PX * 64, 128), F32),
+            pltpu.VMEM((PX, 64, 128), F32),
             pltpu.VMEM((PX, 4, 16, 128), WIRE),
             pltpu.VMEM((PX, 4, 16, 128), WIRE),
             pltpu.VMEM((8, N, 128), WIRE),
@@ -562,9 +581,9 @@
             pltpu.VMEM((frags * 16, 128), BF16),
             pltpu.VMEM((frags, 512), F32),
             pltpu.SemaphoreType.DMA((15,)),
-        ] + [dma] * 8 + [pltpu.SemaphoreType.DMA((6,))],
+        ] + [dma] * 8 + [pltpu.SemaphoreType.DMA((6,)), dma, dma, pltpu.SemaphoreType.DMA((8,))],
         compiler_params=pltpu.CompilerParams(
-            collective_id=0, has_side_effects=True, vmem_limit_bytes=48 * 2**20
+            collective_id=0, has_side_effects=True, vmem_limit_bytes=60 * 2**20
         ),
     )(
         site_charge, corr, solute_pot, chi, home_slab.reshape(1, frags), brick_index.reshape(1, frags),

time: 91.3 us -> 76.5 us (0.84)
  local copies, waits for them, and re-layouts: 13.3 us -> 5.23 us
  Pallas kernels: 76.9 us -> 70.5 us
    unnamed x27 -> x5, local copies, waits for them, and re-layouts: 13.3 us -> 5.23 us
    pallas_call x1, Pallas kernels: 76.9 us -> 70.5 us  [shards(): pl.pallas_call(field_kernel, name='fields', out_shape=(jax.ShapeDtypeStru...]
where the time goes in v4:
time: 76.5 us; the launch traced here: 76.4 us
  Pallas kernels  70.5 us (92%)
  local copies, waits for them, and re-layouts  5.23 us (7%)
    pallas_call x1, Pallas kernels, shards(): pl.pallas_call(field_kernel, name='fields', out_shape=(jax.ShapeDtypeStru...  70.5 us
    unnamed x5, local copies, waits for them, and re-layouts  5.23 us

profile of v4, /device:TPU:1, one launch (start us, length us, event | category | flops | bytes accessed | tf_op | source)
XLA Modules:
  0.0 76.4 jit_solution(6222546448672404823)
XLA Ops:
  0.6 70.5 %fields.1 = (f32[3,8,32,256]{3,2,1,0:T(8,128)}, f32[8,32,256]{2,1,0:T(8,128)}, f32[32,128,128]{2,1,0:T(8,128)}) custom-call(f32[3]{0:T(128)} %charge_ref.1, f32[3,8,32,256]{3,2,1,0:T(8,128)} %corr_hbm.1, bf16[3,8,32,256]{3,2,1,0:T(8,128)(2,1)} %solute_hbm.1, f32[3,3,2,16,8,256]{5,4,3,2,1,0:T(8,128)} %chi_hbm.1, s32[1,32]{1,0:T(1,128)} %bitcast.2, ...), custom_call_target="tpu_custom_call" | custom-call | tf_op jit(solution)/shard_map/fields/pallas_call | solution.py:533
  71.1 0.0 copy-start
  71.1 2.2 %copy.21 = f32[3,8,32,256]{3,2,1,0:T(8,128)} copy(f32[3,8,32,256]{3,2,1,0:T(8,128)} %get-tuple-element.6) | data formatting | bytes 1572864
  73.4 1.7 %copy.22 = f32[8,32,256]{2,1,0:T(8,128)} copy(f32[8,32,256]{2,1,0:T(8,128)} %get-tuple-element.7) | data formatting | bytes 524288
  75.0 0.0 copy-done
  75.0 1.3 %copy.23 = f32[32,128,128]{2,1,0:T(8,128)} copy(f32[32,128,128]{2,1,0:T(8,128)S(1)} %copy-done) | data formatting | bytes 4194304
Async XLA Ops:
  71.1 3.9 %copy-start = (f32[32,128,128]{2,1,0:T(8,128)S(1)}, f32[32,128,128]{2,1,0:T(8,128)}, u32[]{:S(2)}) copy-start(f32[32,128,128]{2,1,0:T(8,128)} %get-tuple-element.8) | copy-start | bytes 6291460

commit v5 on v4

--- a/solution.py
+++ b/solution.py
@@ -44,7 +44,8 @@
     halves = np.stack([half_re.reshape(N, PY, R), half_im.reshape(N, PY, R)], axis=2)
     spread = np.broadcast_to(halves[:, :, :, None, :], (N, PY, 2, FIELDS, R))
     spread = spread.reshape(N, PY * 128)
-    return np_split(spread) + np_split(cos) + np_split(sin)
+    order = index % PX * 8 + index // PX
+    return np_split(spread) + np_split(cos) + np_split(sin) + np_split(cos[:, order]) + np_split(sin[:, order])
 
 
 def encode(values, centre):
@@ -86,14 +87,14 @@
 
 def field_kernel(
     charge_ref, corr_hbm, solute_hbm, chi_hbm, home_hbm, brick_hbm, slot_hbm, basis_hbm, fock_hbm,
-    xh_hbm, xl_hbm, ch_hbm, cl_hbm, sh_hbm, sl_hbm,
+    xh_hbm, xl_hbm, ch_hbm, cl_hbm, sh_hbm, sl_hbm, och_hbm, ocl_hbm, osh_hbm, osl_hbm,
     corr_hbm_out, potential_hbm_out, fock_hbm_out,
     corr_out, potential_out, fock_out,
     corr_ref, solute_ref, chi0, chi1, home_ref, brick_ref, slot_ref, basis_ref, fock_ref,
-    xh_ref, xl_ref, ch_ref, cl_ref, sh_ref, sl_ref,
-    s1, b1, s2, b2, ys, s3, b3, s4, b4,
+    xh_ref, xl_ref, ch_ref, cl_ref, sh_ref, sl_ref, och_ref, ocl_ref, osh_ref, osl_ref,
+    s1, b1, s2, b2, ys, plain_k, turned_k, s3p, b3p, ysp, s4p, b4p, s3, b3, yc, s4, b4,
     ask_out, ask_in, ask_smem, info, info_smem, pot_ref, shuffled, brick_out, brick_in, turned_basis, tiles, samples,
-    in_sem, send1, recv1, send2, recv2, send3, recv3, send4, recv4, brick_sem, corr_sem, potential_sem, fock_sem,
+    in_sem, send1, recv1, send2, recv2, send3, recv3, send4, recv4, pot_sem, brick_sem, corr_sem, potential_sem, fock_sem,
 ):
     px = lax.axis_index("px")
     py = lax.axis_index("py")
@@ -113,6 +114,7 @@
         (home_hbm, home_ref), (brick_hbm, brick_ref), (slot_hbm, slot_ref),
         (chi_hbm.at[:, :, 0], chi0), (chi_hbm.at[:, :, 1, 0], chi1),
         (basis_hbm, basis_ref), (fock_hbm, fock_ref),
+        (och_hbm, och_ref), (ocl_hbm, ocl_ref), (osh_hbm, osh_ref), (osl_hbm, osl_ref),
     )
     loads = [pltpu.make_async_copy(source, to, in_sem.at[i]) for i, (source, to) in enumerate(pairs)]
     for load in loads[:11]:
@@ -243,7 +245,7 @@
 
     lax.fori_loop(0, 4, z_forward, 0)
 
-    def collect(buffer, sem, centre):
+    def collect(buffer, sem, centre, ys, parts):
         def body(part, carry):
             chunk = buffer.at[:, part]
             pltpu.make_async_copy(chunk, chunk, sem.at[part]).wait()
@@ -255,7 +257,7 @@
 
             return lax.fori_loop(0, PX // 8, place, carry)
 
-        lax.fori_loop(0, 4, body, 0)
+        lax.fori_loop(0, parts, body, 0)
 
     pencils = ys.reshape(PX * 64, 128)
 
@@ -265,7 +267,7 @@
 
     loads[13].wait()
     lax.fori_loop(0, 32, turn_basis, 0)
-    collect(b2, recv2, CENTRE_Z)
+    collect(b2, recv2, CENTRE_Z, ys, 4)
     loads[11].wait()
     loads[12].wait()
 
@@ -298,128 +300,176 @@
         out_im.append(pot_im * (screened * scale))
         return out_re, out_im
 
-    def y_both(kp, carry):
-        plain, turned = [], []
-        rows = jnp.concatenate(
-            [pencils[pl.ds(2 * kp + u, N, stride=8), :].T for u in range(2)], axis=0
-        )
-        data = split(rows)
-        cos_data = dot3(dot, data, cos)
-        sin_data = dot3(dot, data, sin)
-        for u in range(2):
-            kz = 2 * kp + u
-            kz_all = px * 8 + kz
-            base = 128 * u
-            pick = lambda array, c, s: array[base + 64 * c + 16 * s:base + 64 * c + 16 * s + 16]
-            c_re = [pick(cos_data, 0, s) for s in range(SITES)]
-            c_im = [pick(cos_data, 1, s) for s in range(SITES)]
-            s_re = [pick(sin_data, 0, s) for s in range(SITES)]
-            s_im = [pick(sin_data, 1, s) for s in range(SITES)]
-            x_re = [c_re[s] + s_im[s] for s in range(SITES)]
-            x_im = [c_im[s] - s_re[s] for s in range(SITES)]
-            upper = first & (kz_all > N // 2)
-            kx = jnp.where(upper, N // 2, py * R + row)
-            square_z = signed_square(jnp.full((1, 1), kz_all, jnp.int32))
-            rest = square_z + square_y + 1.0
-            screened = (4.0 * np.pi) / (signed_square(kx) + rest)
-            chi_of = lambda a, b: jnp.where(upper, chi1[a, b, pl.ds(kz, 1), :], chi0[a, b, :, kz, :])
-            if u == 0:
-                edge = first & ((kz_all == 0) | (kz_all == N // 2))
-                b_re = [c_im[s] for s in range(SITES)]
-                b_im = [-s_im[s] for s in range(SITES)]
-                x_re = [jnp.where(edge, c_re[s], x_re[s]) for s in range(SITES)]
-                x_im = [jnp.where(edge, -s_re[s], x_im[s]) for s in range(SITES)]
-                f_re, f_im = mix(chi_of, x_re, x_im, screened)
-                screened = (4.0 * np.pi) / (np.pi ** 2 + rest)
-                g_re, g_im = mix(lambda a, b: chi1[a, b, pl.ds(kz, 1), :], b_re, b_im, screened)
-                plain += f_re + [jnp.where(edge, g_re[f], f_im[f]) for f in range(FIELDS)]
-                turned += [-value for value in f_im]
-                turned += [jnp.where(edge, -g_im[f], f_re[f]) for f in range(FIELDS)]
-            else:
-                f_re, f_im = mix(chi_of, x_re, x_im, screened)
-                plain += f_re + f_im
-                turned += [-value for value in f_im] + f_re
-        plain = split(jnp.concatenate(plain, axis=0))
-        turned = split(jnp.concatenate(turned, axis=0))
+    def y_forward(quad, carry):
+        for pair in range(2):
+            rows = jnp.concatenate(
+                [pencils[pl.ds(4 * quad + 2 * pair + u, N, stride=8), :].T for u in range(2)], axis=0
+            )
+            data = split(rows)
+            cos_data = dot3(dot, data, cos)
+            sin_data = dot3(dot, data, sin)
+            for u in range(2):
+                k = 2 * pair + u
+                kz = 4 * quad + k
+                kz_all = px * 8 + kz
+                base = 128 * u
+                pick = lambda array, c, s: array[base + 64 * c + 16 * s:base + 64 * c + 16 * s + 16]
+                c_re = [pick(cos_data, 0, s) for s in range(SITES)]
+                c_im = [pick(cos_data, 1, s) for s in range(SITES)]
+                s_re = [pick(sin_data, 0, s) for s in range(SITES)]
+                s_im = [pick(sin_data, 1, s) for s in range(SITES)]
+                x_re = [c_re[s] + s_im[s] for s in range(SITES)]
+                x_im = [c_im[s] - s_re[s] for s in range(SITES)]
+                upper = first & (kz_all > N // 2)
+                kx = jnp.where(upper, N // 2, py * R + row)
+                square_z = signed_square(jnp.full((1, 1), kz_all, jnp.int32))
+                rest = square_z + square_y + 1.0
+                screened = (4.0 * np.pi) / (signed_square(kx) + rest)
+                chi_of = lambda a, b: jnp.where(upper, chi1[a, b, pl.ds(kz, 1), :], chi0[a, b, :, kz, :])
+                if k == 0:
+                    edge = first & ((kz_all == 0) | (kz_all == N // 2))
+                    b_re = [c_im[s] for s in range(SITES)]
+                    b_im = [-s_im[s] for s in range(SITES)]
+                    x_re = [jnp.where(edge, c_re[s], x_re[s]) for s in range(SITES)]
+                    x_im = [jnp.where(edge, -s_re[s], x_im[s]) for s in range(SITES)]
+                    f_re, f_im = mix(chi_of, x_re, x_im, screened)
+                    screened = (4.0 * np.pi) / (np.pi ** 2 + rest)
+                    g_re, g_im = mix(lambda a, b: chi1[a, b, pl.ds(kz, 1), :], b_re, b_im, screened)
+                    other_plain = [jnp.where(edge, g_re[f], f_im[f]) for f in range(FIELDS)]
+                    other_turned = [jnp.where(edge, -g_im[f], f_re[f]) for f in range(FIELDS)]
+                else:
+                    f_re, f_im = mix(chi_of, x_re, x_im, screened)
+                    other_plain, other_turned = f_im, f_re
+                for f in range(FIELDS):
+                    if f == SITES:
+                        group, slot = 6 + quad, k
+                    elif k < 3:
+                        group, slot = 3 * quad + k, f
+                    else:
+                        group, slot = 3 * quad + f, 3
+                    plain_k[group, pl.ds(16 * slot, 16), :] = f_re[f]
+                    plain_k[group, pl.ds(64 + 16 * slot, 16), :] = other_plain[f]
+                    turned_k[group, pl.ds(16 * slot, 16), :] = -f_im[f]
+                    turned_k[group, pl.ds(64 + 16 * slot, 16), :] = other_turned[f]
+        return carry
+
+    lax.fori_loop(0, 2, y_forward, 0)
+
+    def y_backward(unit):
+        groups = pl.ds(2 * unit, 2)
+        plain = split(plain_k[groups].reshape(256, N))
+        turned = split(turned_k[groups].reshape(256, N))
         back = dot3(dot_nt, cos, plain) + dot3(dot_nt, sin, turned)
-        s3[:, kp] = encode(
+        return encode(
             jnp.concatenate([back[:, 128 * u:128 * u + 128].reshape(PX, 8, 128) for u in range(2)], axis=1),
             CENTRE_Y,
         )
-        pltpu.make_async_copy(s3.at[px, kp], b3.at[px, kp], recv3.at[kp]).start()
+
+    s3p[...] = y_backward(3)
+    pltpu.make_async_copy(s3p.at[px], b3p.at[px], pot_sem.at[1]).start()
+
+    def send_potential(step, carry):
+        other = lax.rem(px + step, PX)
+        pltpu.make_async_remote_copy(
+            src_ref=s3p.at[other], dst_ref=b3p.at[px],
+            send_sem=pot_sem.at[0], recv_sem=pot_sem.at[1],
+            device_id=(other, py), device_id_type=MESH,
+        ).start()
+        return carry
+
+    lax.fori_loop(1, PX, send_potential, 0)
+
+    def y_corr(unit, carry):
+        s3[:, unit] = y_backward(unit)
+        pltpu.make_async_copy(s3.at[px, unit], b3.at[px, unit], recv3.at[unit]).start()
 
         def send(step, inner):
             other = lax.rem(px + step, PX)
             pltpu.make_async_remote_copy(
-                src_ref=s3.at[other, kp], dst_ref=b3.at[px, kp],
-                send_sem=send3.at[kp], recv_sem=recv3.at[kp],
+                src_ref=s3.at[other, unit], dst_ref=b3.at[px, unit],
+                send_sem=send3.at[unit], recv_sem=recv3.at[unit],
                 device_id=(other, py), device_id_type=MESH,
             ).start()
             return inner
 
         return lax.fori_loop(1, PX, send, carry)
 
-    lax.fori_loop(0, 4, y_both, 0)
-
-    collect(b3, recv3, CENTRE_Y)
-
-    def z_backward(yp, carry):
+    lax.fori_loop(0, 3, y_corr, 0)
+
+    for load in loads[15:19]:
+        load.wait()
+    cos_order = (och_ref[...], ocl_ref[...])
+    sin_order = (osh_ref[...], osl_ref[...])
+    order = lax.rem(wave, PX) * 8 + wave // PX
+    order_edge = (order == 0) | (order == N // 2)
+    order_low = order < N // 2
+    order_high = order > N // 2
+
+    def z_inverse(columns):
         plain, turned = [], []
-        for u in range(2):
-            data = pencils[pl.ds(2 * yp + u, N, stride=8), :]
+        for data in columns:
             turn = pltpu.roll(data, 64, 1)
-            packed_re = jnp.where(wave_edge, data, jnp.where(wave_low, data + data, 0.0))
-            packed_im = jnp.where(wave_edge, data, jnp.where(wave_low, 0.0, turn + turn))
-            other_re = jnp.where(wave_low & ~wave_edge, -2.0 * turn, 0.0)
-            other_im = jnp.where(wave_high, -2.0 * data, 0.0)
+            packed_re = jnp.where(order_edge, data, jnp.where(order_low, data + data, 0.0))
+            packed_im = jnp.where(order_edge, data, jnp.where(order_low, 0.0, turn + turn))
+            other_re = jnp.where(order_low & ~order_edge, -2.0 * turn, 0.0)
+            other_im = jnp.where(order_high, -2.0 * data, 0.0)
             plain.append(jnp.where(lane_spec, jnp.where(lane_re, packed_re, packed_im), data))
             turned.append(jnp.where(
                 lane_spec, jnp.where(lane_re, other_re, other_im), jnp.where(lane_re, -turn, turn)
             ))
         plain = split(jnp.concatenate(plain, axis=1))
         turned = split(jnp.concatenate(turned, axis=1))
-        back = encode(dot3(dot, cos, plain) + dot3(dot, sin, turned), CENTRE_BACK)
-        s4[2 * yp] = back[:, 0:128]
-        s4[2 * yp + 1] = back[:, 128:256]
-        pltpu.make_async_copy(
-            s4.at[pl.ds(2 * yp, 2), pl.ds(32 * py, 32)], b4.at[py, pl.ds(2 * yp, 2)], recv4.at[yp]
+        return dot3(dot, cos_order, plain) + dot3(dot, sin_order, turned)
+
+    def shift(data, slots):
+        return pltpu.roll(data, 16 * slots % 128, 1) if slots else data
+
+    def x_inverse(rows, count):
+        field = jnp.concatenate([lane_field] * PY, axis=1)
+        data = split(jnp.concatenate([jnp.where(field == f, rows, 0.0) for f in range(count)], axis=0))
+        return dot3(dot_nt, data, (xh_ref[...], xl_ref[...]))
+
+    pltpu.make_async_copy(b3p, b3p, pot_sem.at[1]).wait()
+    ysp[...] = decode(b3p[...], CENTRE_Y)
+    tiles_in = ysp.reshape(PX * 16, 128)
+    columns = []
+    for yq in range(2):
+        parts = []
+        for quad in range(2):
+            rows = [tiles_in[pl.ds(8 * quad + 4 * yq + j, PX, stride=16), :] for j in range(4)]
+            for k in range(4):
+                part = shift(rows[0], -k)
+                for j in range(1, 4):
+                    part = jnp.where(lane_field == j, shift(rows[j], j - k), part)
+                parts.append(part)
+        columns.append(jnp.concatenate(parts, axis=0))
+    back = encode(z_inverse(columns), CENTRE_BACK)
+    s4p[0] = back[:, 0:128]
+    s4p[1] = back[:, 128:256]
+    pltpu.make_async_copy(s4p.at[:, pl.ds(32 * py, 32)], b4p.at[py], pot_sem.at[3]).start()
+
+    def send_rows(step, carry):
+        other = lax.rem(py + step, PY)
+        pltpu.make_async_remote_copy(
+            src_ref=s4p.at[:, pl.ds(32 * other, 32)], dst_ref=b4p.at[py],
+            send_sem=pot_sem.at[2], recv_sem=pot_sem.at[3],
+            device_id=(px, other), device_id_type=MESH,
         ).start()
-
-        def send(step, inner):
-            other = lax.rem(py + step, PY)
-            pltpu.make_async_remote_copy(
-                src_ref=s4.at[pl.ds(2 * yp, 2), pl.ds(32 * other, 32)],
-                dst_ref=b4.at[py, pl.ds(2 * yp, 2)],
-                send_sem=send4.at[yp], recv_sem=recv4.at[yp],
-                device_id=(px, other), device_id_type=MESH,
-            ).start()
-            return inner
-
-        return lax.fori_loop(1, PY, send, carry)
-
-    lax.fori_loop(0, 4, z_backward, 0)
-
-    def x_backward(yp, carry):
-        chunk = b4.at[:, pl.ds(2 * yp, 2)]
-        pltpu.make_async_copy(chunk, chunk, recv4.at[yp]).wait()
-        rows = jnp.concatenate(
-            [decode(b4[j, pl.ds(2 * yp, 2)], CENTRE_BACK).reshape(64, 128) for j in range(PY)], axis=1
-        )
-        field = jnp.concatenate([lane_field] * PY, axis=1)
-        data = split(jnp.concatenate([jnp.where(field == f, rows, 0.0) for f in range(FIELDS)], axis=0))
-        back = dot3(dot_nt, data, (xh_ref[...], xl_ref[...]))
-        for f in range(SITES):
-            corr_out[f, pl.ds(2 * yp, 2)] = back[64 * f:64 * f + 64].reshape(2, 32, N)
-        potential = back[192:256].reshape(2, 32, N)
-        potential_out[pl.ds(2 * yp, 2)] = potential
-        pot_ref[0, pl.ds(2 * yp, 2)] = potential[:, :, 0:128]
-        pot_ref[1, pl.ds(2 * yp, 2)] = potential[:, :, 128:256]
-        slabs = pl.ds(2 * yp, 2)
-        pltpu.make_async_copy(corr_out.at[:, slabs], corr_hbm_out.at[:, slabs], corr_sem.at[yp]).start()
-        pltpu.make_async_copy(potential_out.at[slabs], potential_hbm_out.at[slabs], potential_sem.at[yp]).start()
-        return carry
-
-    lax.fori_loop(0, 4, x_backward, 0)
+        return carry
+
+    lax.fori_loop(1, PY, send_rows, 0)
+    pltpu.make_async_copy(b4p, b4p, pot_sem.at[3]).wait()
+    back = x_inverse(
+        jnp.concatenate([decode(b4p[j], CENTRE_BACK).reshape(64, 128) for j in range(PY)], axis=1), FIELDS
+    )
+    for y in range(8):
+        start = 64 * (y % 4) + 32 * (y // 4)
+        slab = back[start:start + 32]
+        potential_out[y] = slab
+        pot_ref[0, y] = slab[:, 0:128]
+        pot_ref[1, y] = slab[:, 128:256]
+    potential_copy = pltpu.make_async_copy(potential_out, potential_hbm_out, potential_sem.at[0])
+    potential_copy.start()
 
     pltpu.make_async_copy(ask_in, ask_in, brick_sem.at[2]).wait()
     ask_copy = pltpu.make_async_copy(ask_in, ask_smem, brick_sem.at[3])
@@ -469,6 +519,44 @@
 
     lax.fori_loop(0, PX, answer, 0, unroll=2)
     pltpu.make_async_copy(brick_out.at[px], brick_in.at[px], brick_sem.at[5]).start()
+
+    collect(b3, recv3, CENTRE_Y, yc, 3)
+    packed = yc.reshape(PX * 48, 128)
+
+    def z_backward(yp, carry):
+        columns = []
+        for u in range(2):
+            parts = []
+            for quad in range(2):
+                rows = [packed[pl.ds(24 * quad + 8 * g + 2 * yp + u, PX, stride=48), :] for g in range(3)]
+                last = shift(rows[0], -3)
+                for f in range(1, 3):
+                    last = jnp.where(lane_field == f, shift(rows[f], f - 3), last)
+                parts += rows + [last]
+            columns.append(jnp.concatenate(parts, axis=0))
+        back = z_inverse(columns)
+        parts = []
+        for u in range(2):
+            rows = back[:, 128 * u:128 * u + 128].reshape(PY, 4, 8, 128)
+            last = rows[:, 3].reshape(64, 128)
+            for g in range(3):
+                part = jnp.where(lane_field == 3, shift(last, 3 - g), rows[:, g].reshape(64, 128))
+                parts.append(part.reshape(PY, 8, 128))
+        s4[yp] = encode(jnp.concatenate(parts, axis=1), CENTRE_BACK)
+        pltpu.make_async_copy(s4.at[yp, py], b4.at[py, yp], recv4.at[yp]).start()
+
+        def send(step, inner):
+            other = lax.rem(py + step, PY)
+            pltpu.make_async_remote_copy(
+                src_ref=s4.at[yp, other], dst_ref=b4.at[py, yp],
+                send_sem=send4.at[yp], recv_sem=recv4.at[yp],
+                device_id=(px, other), device_id_type=MESH,
+            ).start()
+            return inner
+
+        return lax.fori_loop(1, PY, send, carry)
+
+    lax.fori_loop(0, 4, z_backward, 0)
     info_copy.wait()
     loads[14].wait()
     pltpu.make_async_copy(brick_in, brick_in, brick_sem.at[5]).wait()
@@ -496,16 +584,39 @@
             slot = 4 * group + item
             fragment = info_smem[slot, 0]
             weighted = turned_basis[fragment] * samples[pl.ds(slot, 1), :].astype(BF16)
-            fock_out[slot] = fock_ref[slot] + dot(weighted, basis_ref[fragment])
+            fock_out[slot] = fock_ref[slot] + dot(weighted, basis_ref[fragment]).T
         slots = pl.ds(4 * group, 4)
         pltpu.make_async_copy(fock_out.at[slots], fock_hbm_out.at[slots], fock_sem.at[group]).start()
         return carry
 
     lax.fori_loop(0, 8, embed, 0)
+
+    def x_backward(yp, carry):
+        chunk = b4.at[:, yp]
+        pltpu.make_async_copy(chunk, chunk, recv4.at[yp]).wait()
+        wide = []
+        for j in range(PY):
+            rows = decode(b4[j, yp], CENTRE_BACK)
+            parts = []
+            for u in range(2):
+                three = [rows[24 * u + 8 * g:24 * u + 8 * g + 8] for g in range(3)]
+                last = shift(three[0], -3)
+                for f in range(1, 3):
+                    last = jnp.where(lane_field == f, shift(three[f], f - 3), last)
+                parts += three + [last]
+            wide.append(jnp.concatenate(parts, axis=0))
+        back = x_inverse(jnp.concatenate(wide, axis=1), SITES)
+        slabs = pl.ds(2 * yp, 2)
+        for f in range(SITES):
+            corr_out[f, slabs] = back[64 * f:64 * f + 64].reshape(2, 32, N)
+        pltpu.make_async_copy(corr_out.at[:, slabs], corr_hbm_out.at[:, slabs], corr_sem.at[yp]).start()
+        return carry
+
+    lax.fori_loop(0, 4, x_backward, 0)
+    potential_copy.wait()
     for part in range(4):
         slabs = pl.ds(2 * part, 2)
         pltpu.make_async_copy(corr_out.at[:, slabs], corr_hbm_out.at[:, slabs], corr_sem.at[part]).wait()
-        pltpu.make_async_copy(potential_out.at[slabs], potential_hbm_out.at[slabs], potential_sem.at[part]).wait()
     for part in range(8):
         slots = pl.ds(4 * part, 4)
         pltpu.make_async_copy(fock_out.at[slots], fock_hbm_out.at[slots], fock_sem.at[part]).wait()
@@ -515,9 +626,15 @@
         pltpu.make_async_copy(sent, sent, send1.at[part]).wait()
         sent = s2.at[pl.ds(0, PX - 1), 0]
         pltpu.make_async_copy(sent, sent, send2.at[part]).wait()
-        pltpu.make_async_copy(sent, sent, send3.at[part]).wait()
-        sent = s4.at[pl.ds(0, 2), pl.ds(0, 32 * (PY - 1))]
+        if part < 3:
+            sent = s3.at[pl.ds(0, PX - 1), 0]
+            pltpu.make_async_copy(sent, sent, send3.at[part]).wait()
+        sent = s4.at[0, pl.ds(0, PY - 1)]
         pltpu.make_async_copy(sent, sent, send4.at[part]).wait()
+    sent = s3p.at[pl.ds(0, PX - 1)]
+    pltpu.make_async_copy(sent, sent, pot_sem.at[0]).wait()
+    sent = s4p.at[:, pl.ds(0, 32 * (PY - 1))]
+    pltpu.make_async_copy(sent, sent, pot_sem.at[2]).wait()
     sent = ask_out.at[pl.ds(0, PX - 1)]
     pltpu.make_async_copy(sent, sent, brick_sem.at[1]).wait()
     sent = brick_out.at[pl.ds(0, PX - 1)]
@@ -538,7 +655,7 @@
             jax.ShapeDtypeStruct((8, 32, N), F32),
             jax.ShapeDtypeStruct(fock_in.shape, F32),
         ),
-        in_specs=[pl.BlockSpec(memory_space=pltpu.SMEM)] + [hbm] * 14,
+        in_specs=[pl.BlockSpec(memory_space=pltpu.SMEM)] + [hbm] * 18,
         out_specs=(hbm,) * 3,
         scratch_shapes=[
             pltpu.VMEM(corr.shape, F32),
@@ -555,19 +672,24 @@
             pltpu.VMEM(fock_in.shape, F32),
             pltpu.VMEM((N, PY * 128), BF16),
             pltpu.VMEM((N, PY * 128), BF16),
-            pltpu.VMEM((N, N), BF16),
-            pltpu.VMEM((N, N), BF16),
-            pltpu.VMEM((N, N), BF16),
-            pltpu.VMEM((N, N), BF16),
+        ] + [pltpu.VMEM((N, N), BF16)] * 8 + [
             pltpu.VMEM((PY, 8, 32, 128), WIRE),
             pltpu.VMEM((8, N, 128), WIRE),
             pltpu.VMEM((PX, 4, 16, 128), WIRE),
             pltpu.VMEM((PX, 4, 16, 128), WIRE),
             pltpu.VMEM((PX, 64, 128), F32),
-            pltpu.VMEM((PX, 4, 16, 128), WIRE),
-            pltpu.VMEM((PX, 4, 16, 128), WIRE),
-            pltpu.VMEM((8, N, 128), WIRE),
-            pltpu.VMEM((PY, 8, 32, 128), WIRE),
+            pltpu.VMEM((8, 128, N), F32),
+            pltpu.VMEM((8, 128, N), F32),
+            pltpu.VMEM((PX, 16, 128), WIRE),
+            pltpu.VMEM((PX, 16, 128), WIRE),
+            pltpu.VMEM((PX, 16, 128), F32),
+            pltpu.VMEM((2, N, 128), WIRE),
+            pltpu.VMEM((PY, 2, 32, 128), WIRE),
+            pltpu.VMEM((PX, 3, 16, 128), WIRE),
+            pltpu.VMEM((PX, 3, 16, 128), WIRE),
+            pltpu.VMEM((PX, 48, 128), F32),
+            pltpu.VMEM((4, PY, 48, 128), WIRE),
+            pltpu.VMEM((PY, 4, 48, 128), WIRE),
             pltpu.VMEM((PX, 1, 128), jnp.int32),
             pltpu.VMEM((PX, 1, 128), jnp.int32),
             pltpu.SMEM((PX, 1, 128), jnp.int32),
@@ -580,8 +702,8 @@
             pltpu.VMEM((frags, 128, 512), BF16),
             pltpu.VMEM((frags * 16, 128), BF16),
             pltpu.VMEM((frags, 512), F32),
-            pltpu.SemaphoreType.DMA((15,)),
-        ] + [dma] * 8 + [pltpu.SemaphoreType.DMA((6,)), dma, dma, pltpu.SemaphoreType.DMA((8,))],
+            pltpu.SemaphoreType.DMA((19,)),
+        ] + [dma] * 9 + [pltpu.SemaphoreType.DMA((6,)), dma, dma, pltpu.SemaphoreType.DMA((8,))],
         compiler_params=pltpu.CompilerParams(
             collective_id=0, has_side_effects=True, vmem_limit_bytes=60 * 2**20
         ),

time: 76.5 us -> 72.1 us (0.942)
  Pallas kernels: 70.5 us -> 66.1 us
    pallas_call x1, Pallas kernels: 70.5 us -> 66.1 us  [shards(): pl.pallas_call(field_kernel, name='fields', out_shape=(jax.ShapeDtypeStru...]
where the time goes in v5:
time: 72.1 us; the launch traced here: 72 us
  Pallas kernels  66.1 us (92%)
  local copies, waits for them, and re-layouts  5.23 us (7%)
    pallas_call x1, Pallas kernels, shards(): pl.pallas_call(field_kernel, name='fields', out_shape=(jax.ShapeDtypeStru...  66.1 us
    unnamed x5, local copies, waits for them, and re-layouts  5.23 us

profile of v5, /device:TPU:1, one launch (start us, length us, event | category | flops | bytes accessed | tf_op | source)
XLA Modules:
  0.0 72.0 jit_solution(13239264550765477451)
XLA Ops:
  0.6 66.1 %fields.1 = (f32[3,8,32,256]{3,2,1,0:T(8,128)}, f32[8,32,256]{2,1,0:T(8,128)}, f32[32,128,128]{2,1,0:T(8,128)}) custom-call(f32[3]{0:T(128)} %charge_ref.1, f32[3,8,32,256]{3,2,1,0:T(8,128)} %corr_hbm.1, bf16[3,8,32,256]{3,2,1,0:T(8,128)(2,1)} %solute_hbm.1, f32[3,3,2,16,8,256]{5,4,3,2,1,0:T(8,128)} %chi_hbm.1, s32[1,32]{1,0:T(1,128)} %bitcast.2, ...), custom_call_target="tpu_custom_call" | custom-call | tf_op jit(solution)/shard_map/fields/pallas_call | solution.py:650
  66.7 0.0 copy-start
  66.8 2.2 %copy.25 = f32[3,8,32,256]{3,2,1,0:T(8,128)} copy(f32[3,8,32,256]{3,2,1,0:T(8,128)} %get-tuple-element.6) | data formatting | bytes 1572864
  69.0 1.7 %copy.26 = f32[8,32,256]{2,1,0:T(8,128)} copy(f32[8,32,256]{2,1,0:T(8,128)} %get-tuple-element.7) | data formatting | bytes 524288
  70.7 0.0 copy-done
  70.7 1.3 %copy.27 = f32[32,128,128]{2,1,0:T(8,128)} copy(f32[32,128,128]{2,1,0:T(8,128)S(1)} %copy-done) | data formatting | bytes 4194304
Async XLA Ops:
  66.7 3.9 %copy-start = (f32[32,128,128]{2,1,0:T(8,128)S(1)}, f32[32,128,128]{2,1,0:T(8,128)}, u32[]{:S(2)}) copy-start(f32[32,128,128]{2,1,0:T(8,128)} %get-tuple-element.8) | copy-start | bytes 6291460

commit v6 on v5

--- a/solution.py
+++ b/solution.py
@@ -92,7 +92,7 @@
     corr_out, potential_out, fock_out,
     corr_ref, solute_ref, chi0, chi1, home_ref, brick_ref, slot_ref, basis_ref, fock_ref,
     xh_ref, xl_ref, ch_ref, cl_ref, sh_ref, sl_ref, och_ref, ocl_ref, osh_ref, osl_ref,
-    s1, b1, s2, b2, ys, plain_k, turned_k, s3p, b3p, ysp, s4p, b4p, s3, b3, yc, s4, b4,
+    s1, b1, s2, b2, ys, plain_k, turned_k, s3p, b3p, ysp, s4p, b4p, s3, b3, yc, s4, b4, weights,
     ask_out, ask_in, ask_smem, info, info_smem, pot_ref, shuffled, brick_out, brick_in, turned_basis, tiles, samples,
     in_sem, send1, recv1, send2, recv2, send3, recv3, send4, recv4, pot_sem, brick_sem, corr_sem, potential_sem, fock_sem,
 ):
@@ -405,18 +405,21 @@
     order_low = order < N // 2
     order_high = order > N // 2
 
+    zero, one, two = jnp.zeros((N, 128), F32), jnp.ones((N, 128), F32), jnp.full((N, 128), 2.0, F32)
+    packed_re = jnp.where(order_edge, one, jnp.where(order_low, two, zero))
+    packed_im = jnp.where(order_edge, one, zero)
+    weights[0] = jnp.where(lane_spec, jnp.where(lane_re, packed_re, packed_im), one)
+    weights[1] = jnp.where(lane_spec & ~lane_re & order_high, two, zero)
+    weights[2] = jnp.where(lane_spec & ~lane_re & order_high, -two, zero)
+    usual = jnp.where(lane_re, -one, one)
+    weights[3] = jnp.where(lane_spec, jnp.where(lane_re & order_low & ~order_edge, -two, zero), usual)
+
     def z_inverse(columns):
         plain, turned = [], []
         for data in columns:
             turn = pltpu.roll(data, 64, 1)
-            packed_re = jnp.where(order_edge, data, jnp.where(order_low, data + data, 0.0))
-            packed_im = jnp.where(order_edge, data, jnp.where(order_low, 0.0, turn + turn))
-            other_re = jnp.where(order_low & ~order_edge, -2.0 * turn, 0.0)
-            other_im = jnp.where(order_high, -2.0 * data, 0.0)
-            plain.append(jnp.where(lane_spec, jnp.where(lane_re, packed_re, packed_im), data))
-            turned.append(jnp.where(
-                lane_spec, jnp.where(lane_re, other_re, other_im), jnp.where(lane_re, -turn, turn)
-            ))
+            plain.append(data * weights[0] + turn * weights[1])
+            turned.append(data * weights[2] + turn * weights[3])
         plain = split(jnp.concatenate(plain, axis=1))
         turned = split(jnp.concatenate(turned, axis=1))
         return dot3(dot, cos_order, plain) + dot3(dot, sin_order, turned)
@@ -517,7 +520,7 @@
 
         return carry
 
-    lax.fori_loop(0, PX, answer, 0, unroll=2)
+    lax.fori_loop(0, PX, answer, 0, unroll=4)
     pltpu.make_async_copy(brick_out.at[px], brick_in.at[px], brick_sem.at[5]).start()
 
     collect(b3, recv3, CENTRE_Y, yc, 3)
@@ -567,7 +570,7 @@
         tiles[pl.ds(pl.multiple_of(16 * slot, 16), 16), :] = tile.astype(BF16)
         return carry
 
-    lax.fori_loop(0, 32, take, 0, unroll=4)
+    lax.fori_loop(0, 32, take, 0, unroll=8)
     cell = lax.broadcasted_iota(jnp.int32, (128, 512), 1)
     origin = lax.broadcasted_iota(jnp.int32, (128, 512), 0)
     spread = (origin == 32 * (cell // 128) + lax.rem(cell, BRICK)).astype(F32).astype(BF16)
@@ -641,13 +644,33 @@
     pltpu.make_async_copy(sent, sent, brick_sem.at[4]).wait()
 
 
+def store_kernel(*refs):
+    sources, targets, held, in_sem, out_sem = refs[:3], refs[3:6], refs[6:9], refs[9], refs[10]
+    loads, stores = [], []
+    for i in range(3):
+        count = (3, 1, 8)[i]
+        step = sources[i].shape[0] // count
+        for part in range(count):
+            rows = pl.ds(part * step, step)
+            sem = len(loads)
+            loads.append(pltpu.make_async_copy(sources[i].at[rows], held[i].at[rows], in_sem.at[sem]))
+            stores.append(pltpu.make_async_copy(held[i].at[rows], targets[i].at[rows], out_sem.at[sem]))
+    for load in loads:
+        load.start()
+    for load, store in zip(loads, stores):
+        load.wait()
+        store.start()
+    for store in stores:
+        store.wait()
+
+
 def shards(
     corr, solute_pot, chi, site_charge, home_slab, brick_index, block_slot, basis_values, fock_in
 ):
     hbm = pl.BlockSpec(memory_space=pltpu.HBM)
     dma = pltpu.SemaphoreType.DMA((4,))
     frags = home_slab.shape[0]
-    return pl.pallas_call(
+    results = pl.pallas_call(
         field_kernel,
         name="fields",
         out_shape=(
@@ -690,6 +713,7 @@
             pltpu.VMEM((PX, 48, 128), F32),
             pltpu.VMEM((4, PY, 48, 128), WIRE),
             pltpu.VMEM((PY, 4, 48, 128), WIRE),
+            pltpu.VMEM((4, N, 128), F32),
             pltpu.VMEM((PX, 1, 128), jnp.int32),
             pltpu.VMEM((PX, 1, 128), jnp.int32),
             pltpu.SMEM((PX, 1, 128), jnp.int32),
@@ -711,6 +735,16 @@
         site_charge, corr, solute_pot, chi, home_slab.reshape(1, frags), brick_index.reshape(1, frags),
         block_slot, basis_values, fock_in, *[jnp.asarray(table) for table in tables()],
     )
+    shapes = [jax.ShapeDtypeStruct(result.shape, F32) for result in results]
+    return pl.pallas_call(
+        store_kernel,
+        name="store",
+        out_shape=tuple(shapes),
+        in_specs=[hbm] * 3,
+        out_specs=(hbm,) * 3,
+        scratch_shapes=[pltpu.VMEM(shape.shape, F32) for shape in shapes] + [pltpu.SemaphoreType.DMA((12,))] * 2,
+        compiler_params=pltpu.CompilerParams(vmem_limit_bytes=60 * 2**20),
+    )(*results)
 
 
 def solution(mesh):

time: 72.1 us -> 68.9 us (0.956)
  local copies, waits for them, and re-layouts: 5.23 us -> 0 us
  Pallas kernels: 66.1 us -> 68.2 us
    unnamed x5 -> x0, local copies, waits for them, and re-layouts: 5.23 us -> none
    pallas_call x0 -> x1, Pallas kernels: none -> 2.81 us  [shards(): pl.pallas_call(store_kernel, name='store', out_shape=tuple(shapes), in_sp...]
    pallas_call x1, Pallas kernels: 66.1 us -> 65.3 us  [shards(): pl.pallas_call(field_kernel, name='fields', out_shape=(jax.ShapeDtypeStru...]
where the time goes in v6:
time: 68.9 us; the launch traced here: 68.8 us
  Pallas kernels  68.2 us (99%)
    pallas_call x1, Pallas kernels, shards(): pl.pallas_call(field_kernel, name='fields', out_shape=(jax.ShapeDtypeStru...  65.3 us
    pallas_call x1, Pallas kernels, shards(): pl.pallas_call(store_kernel, name='store', out_shape=tuple(shapes), in_sp...  2.81 us

profile of v6, /device:TPU:1, one launch (start us, length us, event | category | flops | bytes accessed | tf_op | source)
XLA Modules:
  0.0 68.8 jit_solution(7374849380240711642)
XLA Ops:
  0.6 65.3 %fields.1 = (f32[3,8,32,256]{3,2,1,0:T(8,128)}, f32[8,32,256]{2,1,0:T(8,128)}, f32[32,128,128]{2,1,0:T(8,128)}) custom-call(f32[3]{0:T(128)} %charge_ref.1, f32[3,8,32,256]{3,2,1,0:T(8,128)} %corr_hbm.1, bf16[3,8,32,256]{3,2,1,0:T(8,128)(2,1)} %solute_hbm.1, f32[3,3,2,16,8,256]{5,4,3,2,1,0:T(8,128)} %chi_hbm.1, s32[1,32]{1,0:T(1,128)} %bitcast.2, ...), custom_call_target="tpu_custom_call" | custom-call | tf_op jit(solution)/shard_map/fields/pallas_call | solution.py:673
  66.0 2.8 %store.1 = (f32[3,8,32,256]{3,2,1,0:T(8,128)}, f32[8,32,256]{2,1,0:T(8,128)}, f32[32,128,128]{2,1,0:T(8,128)}) custom-call(f32[3,8,32,256]{3,2,1,0:T(8,128)} %get-tuple-element.6.refs_0_, f32[8,32,256]{2,1,0:T(8,128)} %get-tuple-element.7.refs_1_, f32[32,128,128]{2,1,0:T(8,128)} %get-tuple-element.8.refs_2_), custom_call_target="tpu_custom_call" | custom-call | tf_op jit(solution)/shard_map/store/pallas_call | solution.py:739

commit v7 on v6

--- a/solution.py
+++ b/solution.py
@@ -92,7 +92,7 @@
     corr_out, potential_out, fock_out,
     corr_ref, solute_ref, chi0, chi1, home_ref, brick_ref, slot_ref, basis_ref, fock_ref,
     xh_ref, xl_ref, ch_ref, cl_ref, sh_ref, sl_ref, och_ref, ocl_ref, osh_ref, osl_ref,
-    s1, b1, s2, b2, ys, plain_k, turned_k, s3p, b3p, ysp, s4p, b4p, s3, b3, yc, s4, b4, weights,
+    s1, b1, s2, b2, held, ys, plain_k, turned_k, s3p, b3p, ysp, s4p, b4p, s3, b3, yc, s4, b4, weights,
     ask_out, ask_in, ask_smem, info, info_smem, pot_ref, shuffled, brick_out, brick_in, turned_basis, tiles, samples,
     in_sem, send1, recv1, send2, recv2, send3, recv3, send4, recv4, pot_sem, brick_sem, corr_sem, potential_sem, fock_sem,
 ):
@@ -131,9 +131,22 @@
     lane_field = lax.rem(lane // R, FIELDS)
     lane_spec = (lax.rem(lane, R) == 0) & (py == 0)
 
+    def shift(data, slots):
+        return pltpu.roll(data, 16 * slots % 128, 1) if slots else data
+
+    def pack(parts):
+        return [jnp.where(lane_field == 3, shift(parts[3], 3 - g), parts[g]) for g in range(3)]
+
+    def unpack(parts):
+        last = shift(parts[0], -3)
+        for f in range(1, 3):
+            last = jnp.where(lane_field == f, shift(parts[f], f - 3), last)
+        return parts + [last]
+
     lane_site = jnp.concatenate([lane_field, lane_field], axis=1)
 
-    def x_forward(yp, carry):
+    def x_forward(turn, carry):
+        yp = lax.rem(turn + 3, 4)
         parts = []
         for site in range(SITES):
             rows = closure(corr_ref[site, pl.ds(2 * yp, 2)], solute_ref[site, pl.ds(2 * yp, 2)])
@@ -142,23 +155,24 @@
         for pair in range(PY // 2):
             wide = dot3(dot, data, (xh_ref[:, 256 * pair:256 * pair + 256], xl_ref[:, 256 * pair:256 * pair + 256]))
             rows = jnp.where(lane_site == 0, wide[0:64], jnp.where(lane_site == 1, wide[64:128], wide[128:192]))
-            rows = encode(jnp.where(lane_site == 3, 0.0, rows), CENTRE_X)
-            s1[2 * pair, pl.ds(2 * yp, 2)] = rows[:, 0:128].reshape(2, 32, 128)
-            s1[2 * pair + 1, pl.ds(2 * yp, 2)] = rows[:, 128:256].reshape(2, 32, 128)
-
-        @pl.when(yp == 0)
+            for half in range(2):
+                part = rows[:, 128 * half:128 * half + 128]
+                packed = pack([part[8 * g:8 * g + 8] for g in range(4)])
+                packed += pack([part[32 + 8 * g:40 + 8 * g] for g in range(4)])
+                s1[2 * pair + half, yp] = encode(jnp.concatenate(packed, axis=0), CENTRE_X)
+
+        @pl.when(turn == 0)
         def _():
             pl.semaphore_wait(barrier, PX + PY - 2)
 
         pltpu.make_async_copy(
-            s1.at[py, pl.ds(2 * yp, 2)], b1.at[pl.ds(2 * yp, 2), pl.ds(32 * py, 32)], recv1.at[yp]
+            s1.at[py, yp], b1.at[py, yp], recv1.at[yp]
         ).start()
 
         def send(step, inner):
             other = lax.rem(py + step, PY)
             pltpu.make_async_remote_copy(
-                src_ref=s1.at[other, pl.ds(2 * yp, 2)],
-                dst_ref=b1.at[pl.ds(2 * yp, 2), pl.ds(32 * py, 32)],
+                src_ref=s1.at[other, yp], dst_ref=b1.at[py, yp],
                 send_sem=send1.at[yp], recv_sem=recv1.at[yp],
                 device_id=(px, other), device_id_type=MESH,
             ).start()
@@ -212,10 +226,15 @@
     wave_low = wave < N // 2
     wave_high = wave > N // 2
 
-    def z_forward(yp, carry):
-        chunk = b1.at[pl.ds(2 * yp, 2)]
+    def z_forward(yp):
+        chunk = b1.at[:, yp]
         pltpu.make_async_copy(chunk, chunk, recv1.at[yp]).wait()
-        data = split(jnp.concatenate([decode(b1[2 * yp + u], CENTRE_X) for u in range(2)], axis=1))
+        columns = [[], []]
+        for j in range(PY):
+            rows = decode(b1[j, yp], CENTRE_X)
+            for u in range(2):
+                columns[u] += unpack([rows[24 * u + 8 * g:24 * u + 8 * g + 8] for g in range(3)])
+        data = split(jnp.concatenate([jnp.concatenate(column, axis=0) for column in columns], axis=1))
         cos_data = dot3(dot, cos, data)
         sin_data = dot3(dot, sin, data)
         halves = []
@@ -229,7 +248,14 @@
             packed_im = jnp.where(wave_edge, cd, jnp.where(wave_low, -sd_turn, -sd))
             packed = jnp.where(lane_re, packed_re, packed_im)
             halves.append(jnp.where(lane_spec, packed, usual).reshape(PX, 8, 128))
-        s2[:, yp] = encode(jnp.concatenate(halves, axis=1), CENTRE_Z)
+        return jnp.concatenate(halves, axis=1)
+
+    held[...] = z_forward(3)
+
+    def z_send(yp, carry):
+        rows = z_forward(yp).reshape(PX * 16, 128)
+        moved = pltpu.roll(held[...].reshape(PX * 16, 128), 48 - 16 * yp, 1)
+        s2[:, yp] = encode(jnp.where(lane_field == 3, moved, rows), CENTRE_Z).reshape(PX, 16, 128)
         pltpu.make_async_copy(s2.at[px, yp], b2.at[px, yp], recv2.at[yp]).start()
 
         def send(step, inner):
@@ -243,7 +269,7 @@
 
         return lax.fori_loop(1, PX, send, carry)
 
-    lax.fori_loop(0, 4, z_forward, 0)
+    lax.fori_loop(0, 3, z_send, 0)
 
     def collect(buffer, sem, centre, ys, parts):
         def body(part, carry):
@@ -267,7 +293,15 @@
 
     loads[13].wait()
     lax.fori_loop(0, 32, turn_basis, 0)
-    collect(b2, recv2, CENTRE_Z, ys, 4)
+    collect(b2, recv2, CENTRE_Z, ys, 3)
+
+    def unfold(group, carry):
+        sources = pl.ds(8 * group, 8)
+        rows = [ys[sources, 16 * part:16 * part + 16, :].reshape(128, 128) for part in range(3)]
+        ys[sources, 48:64, :] = unpack(rows)[3].reshape(8, 16, 128)
+        return carry
+
+    lax.fori_loop(0, PX // 8, unfold, 0)
     loads[11].wait()
     loads[12].wait()
 
@@ -424,12 +458,10 @@
         turned = split(jnp.concatenate(turned, axis=1))
         return dot3(dot, cos_order, plain) + dot3(dot, sin_order, turned)
 
-    def shift(data, slots):
-        return pltpu.roll(data, 16 * slots % 128, 1) if slots else data
-
     def x_inverse(rows, count):
         field = jnp.concatenate([lane_field] * PY, axis=1)
-        data = split(jnp.concatenate([jnp.where(field == f, rows, 0.0) for f in range(count)], axis=0))
+        masks = [(field == f).astype(F32).astype(BF16) for f in range(count)]
+        data = [jnp.concatenate([part * mask for mask in masks], axis=0) for part in split(rows)]
         return dot3(dot_nt, data, (xh_ref[...], xl_ref[...]))
 
     pltpu.make_async_copy(b3p, b3p, pot_sem.at[1]).wait()
@@ -532,19 +564,13 @@
             parts = []
             for quad in range(2):
                 rows = [packed[pl.ds(24 * quad + 8 * g + 2 * yp + u, PX, stride=48), :] for g in range(3)]
-                last = shift(rows[0], -3)
-                for f in range(1, 3):
-                    last = jnp.where(lane_field == f, shift(rows[f], f - 3), last)
-                parts += rows + [last]
+                parts += unpack(rows)
             columns.append(jnp.concatenate(parts, axis=0))
         back = z_inverse(columns)
         parts = []
         for u in range(2):
             rows = back[:, 128 * u:128 * u + 128].reshape(PY, 4, 8, 128)
-            last = rows[:, 3].reshape(64, 128)
-            for g in range(3):
-                part = jnp.where(lane_field == 3, shift(last, 3 - g), rows[:, g].reshape(64, 128))
-                parts.append(part.reshape(PY, 8, 128))
+            parts += [part.reshape(PY, 8, 128) for part in pack([rows[:, g].reshape(64, 128) for g in range(4)])]
         s4[yp] = encode(jnp.concatenate(parts, axis=1), CENTRE_BACK)
         pltpu.make_async_copy(s4.at[yp, py], b4.at[py, yp], recv4.at[yp]).start()
 
@@ -602,11 +628,7 @@
             rows = decode(b4[j, yp], CENTRE_BACK)
             parts = []
             for u in range(2):
-                three = [rows[24 * u + 8 * g:24 * u + 8 * g + 8] for g in range(3)]
-                last = shift(three[0], -3)
-                for f in range(1, 3):
-                    last = jnp.where(lane_field == f, shift(three[f], f - 3), last)
-                parts += three + [last]
+                parts += unpack([rows[24 * u + 8 * g:24 * u + 8 * g + 8] for g in range(3)])
             wide.append(jnp.concatenate(parts, axis=0))
         back = x_inverse(jnp.concatenate(wide, axis=1), SITES)
         slabs = pl.ds(2 * yp, 2)
@@ -625,11 +647,11 @@
         pltpu.make_async_copy(fock_out.at[slots], fock_hbm_out.at[slots], fock_sem.at[part]).wait()
 
     for part in range(4):
-        sent = s1.at[pl.ds(0, PY - 1), pl.ds(0, 2)]
+        sent = s1.at[pl.ds(0, PY - 1), 0]
         pltpu.make_async_copy(sent, sent, send1.at[part]).wait()
-        sent = s2.at[pl.ds(0, PX - 1), 0]
-        pltpu.make_async_copy(sent, sent, send2.at[part]).wait()
         if part < 3:
+            sent = s2.at[pl.ds(0, PX - 1), 0]
+            pltpu.make_async_copy(sent, sent, send2.at[part]).wait()
             sent = s3.at[pl.ds(0, PX - 1), 0]
             pltpu.make_async_copy(sent, sent, send3.at[part]).wait()
         sent = s4.at[0, pl.ds(0, PY - 1)]
@@ -696,10 +718,11 @@
             pltpu.VMEM((N, PY * 128), BF16),
             pltpu.VMEM((N, PY * 128), BF16),
         ] + [pltpu.VMEM((N, N), BF16)] * 8 + [
-            pltpu.VMEM((PY, 8, 32, 128), WIRE),
-            pltpu.VMEM((8, N, 128), WIRE),
-            pltpu.VMEM((PX, 4, 16, 128), WIRE),
-            pltpu.VMEM((PX, 4, 16, 128), WIRE),
+            pltpu.VMEM((PY, 4, 48, 128), WIRE),
+            pltpu.VMEM((PY, 4, 48, 128), WIRE),
+            pltpu.VMEM((PX, 3, 16, 128), WIRE),
+            pltpu.VMEM((PX, 3, 16, 128), WIRE),
+            pltpu.VMEM((PX, 16, 128), F32),
             pltpu.VMEM((PX, 64, 128), F32),
             pltpu.VMEM((8, 128, N), F32),
             pltpu.VMEM((8, 128, N), F32),

time: 68.9 us -> 67.5 us (0.980)
  Pallas kernels: 68.2 us -> 66.7 us
    pallas_call x1, Pallas kernels: 65.3 us -> 63.9 us  [shards(): pl.pallas_call(field_kernel, name='fields', out_shape=(jax.ShapeDtypeStru...]
where the time goes in v7:
time: 67.5 us; the launch traced here: 67.4 us
  Pallas kernels  66.7 us (99%)
    pallas_call x1, Pallas kernels, shards(): pl.pallas_call(field_kernel, name='fields', out_shape=(jax.ShapeDtypeStru...  63.9 us
    pallas_call x1, Pallas kernels, shards(): pl.pallas_call(store_kernel, name='store', out_shape=tuple(shapes), in_sp...  2.81 us

profile of v7, /device:TPU:1, one launch (start us, length us, event | category | flops | bytes accessed | tf_op | source)
XLA Modules:
  0.0 67.4 jit_solution(14300862013219994040)
XLA Ops:
  0.6 63.9 %fields.1 = (f32[3,8,32,256]{3,2,1,0:T(8,128)}, f32[8,32,256]{2,1,0:T(8,128)}, f32[32,128,128]{2,1,0:T(8,128)}) custom-call(f32[3]{0:T(128)} %charge_ref.1, f32[3,8,32,256]{3,2,1,0:T(8,128)} %corr_hbm.1, bf16[3,8,32,256]{3,2,1,0:T(8,128)(2,1)} %solute_hbm.1, f32[3,3,2,16,8,256]{5,4,3,2,1,0:T(8,128)} %chi_hbm.1, s32[1,32]{1,0:T(1,128)} %bitcast.2, ...), custom_call_target="tpu_custom_call" | custom-call | tf_op jit(solution)/shard_map/fields/pallas_call | solution.py:695
  64.6 2.8 %store.1 = (f32[3,8,32,256]{3,2,1,0:T(8,128)}, f32[8,32,256]{2,1,0:T(8,128)}, f32[32,128,128]{2,1,0:T(8,128)}) custom-call(f32[3,8,32,256]{3,2,1,0:T(8,128)} %get-tuple-element.6.refs_0_, f32[8,32,256]{2,1,0:T(8,128)} %get-tuple-element.7.refs_1_, f32[32,128,128]{2,1,0:T(8,128)} %get-tuple-element.8.refs_2_), custom_call_target="tpu_custom_call" | custom-call | tf_op jit(solution)/shard_map/store/pallas_call | solution.py:762

commit v8 on v7

--- a/solution.py
+++ b/solution.py
@@ -99,6 +99,9 @@
     px = lax.axis_index("px")
     py = lax.axis_index("py")
     barrier = pltpu.get_barrier_semaphore()
+
+    def far(step):
+        return lax.rem(px + PX // 2 + (step // 2) * (2 * lax.rem(step, 2) - 1) + PX, PX)
 
     def greet_px(step, carry):
         pl.semaphore_signal(barrier, inc=1, device_id=(lax.rem(px + step, PX), py), device_id_type=MESH)
@@ -207,7 +210,7 @@
     pltpu.make_async_copy(ask_out.at[px], ask_in.at[px], brick_sem.at[2]).start()
 
     def ask(step, carry):
-        other = lax.rem(px + step, PX)
+        other = far(step)
         pltpu.make_async_remote_copy(
             src_ref=ask_out.at[other], dst_ref=ask_in.at[px],
             send_sem=brick_sem.at[1], recv_sem=brick_sem.at[2],
@@ -259,7 +262,7 @@
         pltpu.make_async_copy(s2.at[px, yp], b2.at[px, yp], recv2.at[yp]).start()
 
         def send(step, inner):
-            other = lax.rem(px + step, PX)
+            other = far(step)
             pltpu.make_async_remote_copy(
                 src_ref=s2.at[other, yp], dst_ref=b2.at[px, yp],
                 send_sem=send2.at[yp], recv_sem=recv2.at[yp],
@@ -403,7 +406,7 @@
     pltpu.make_async_copy(s3p.at[px], b3p.at[px], pot_sem.at[1]).start()
 
     def send_potential(step, carry):
-        other = lax.rem(px + step, PX)
+        other = far(step)
         pltpu.make_async_remote_copy(
             src_ref=s3p.at[other], dst_ref=b3p.at[px],
             send_sem=pot_sem.at[0], recv_sem=pot_sem.at[1],
@@ -418,7 +421,7 @@
         pltpu.make_async_copy(s3.at[px, unit], b3.at[px, unit], recv3.at[unit]).start()
 
         def send(step, inner):
-            other = lax.rem(px + step, PX)
+            other = far(step)
             pltpu.make_async_remote_copy(
                 src_ref=s3.at[other, unit], dst_ref=b3.at[px, unit],
                 send_sem=send3.at[unit], recv_sem=recv3.at[unit],
@@ -533,8 +536,7 @@
     ask_copy.wait()
     lane_place = lax.rem(lane // BRICK, MOST)
 
-    def answer(step, carry):
-        other = lax.rem(px + step, PX)
+    def fill(other):
         tile = jnp.zeros((16, 128), F32)
         for k in range(MOST):
             index = ask_smem[other, 0, k]
@@ -542,17 +544,18 @@
             tile = jnp.where(lane_place == k, moved, tile)
         brick_out[other] = tile.astype(BF16)
 
-        @pl.when(step > 0)
-        def _():
-            pltpu.make_async_remote_copy(
-                src_ref=brick_out.at[other], dst_ref=brick_in.at[px],
-                send_sem=brick_sem.at[4], recv_sem=brick_sem.at[5],
-                device_id=(other, py), device_id_type=MESH,
-            ).start()
-
-        return carry
-
-    lax.fori_loop(0, PX, answer, 0, unroll=4)
+    def answer(step, carry):
+        other = far(step)
+        fill(other)
+        pltpu.make_async_remote_copy(
+            src_ref=brick_out.at[other], dst_ref=brick_in.at[px],
+            send_sem=brick_sem.at[4], recv_sem=brick_sem.at[5],
+            device_id=(other, py), device_id_type=MESH,
+        ).start()
+        return carry
+
+    lax.fori_loop(1, PX, answer, 0, unroll=2)
+    fill(px)
     pltpu.make_async_copy(brick_out.at[px], brick_in.at[px], brick_sem.at[5]).start()
 
     collect(b3, recv3, CENTRE_Y, yc, 3)

time: 67.5 us -> 65.8 us (0.975)
  Pallas kernels: 66.7 us -> 65 us
    pallas_call x1, Pallas kernels: 63.9 us -> 62.2 us  [shards(): pl.pallas_call(field_kernel, name='fields', out_shape=(jax.ShapeDtypeStru...]
where the time goes in v8:
time: 65.8 us; the launch traced here: 65.7 us
  Pallas kernels  65 us (99%)
    pallas_call x1, Pallas kernels, shards(): pl.pallas_call(field_kernel, name='fields', out_shape=(jax.ShapeDtypeStru...  62.2 us
    pallas_call x1, Pallas kernels, shards(): pl.pallas_call(store_kernel, name='store', out_shape=tuple(shapes), in_sp...  2.81 us

profile of v8, /device:TPU:1, one launch (start us, length us, event | category | flops | bytes accessed | tf_op | source)
XLA Modules:
  0.0 65.7 jit_solution(18043548179612814874)
XLA Ops:
  0.6 62.2 %fields.1 = (f32[3,8,32,256]{3,2,1,0:T(8,128)}, f32[8,32,256]{2,1,0:T(8,128)}, f32[32,128,128]{2,1,0:T(8,128)}) custom-call(f32[3]{0:T(128)} %charge_ref.1, f32[3,8,32,256]{3,2,1,0:T(8,128)} %corr_hbm.1, bf16[3,8,32,256]{3,2,1,0:T(8,128)(2,1)} %solute_hbm.1, f32[3,3,2,16,8,256]{5,4,3,2,1,0:T(8,128)} %chi_hbm.1, s32[1,32]{1,0:T(1,128)} %bitcast.2, ...), custom_call_target="tpu_custom_call" | custom-call | tf_op jit(solution)/shard_map/fields/pallas_call | solution.py:698
  62.9 2.8 %store.1 = (f32[3,8,32,256]{3,2,1,0:T(8,128)}, f32[8,32,256]{2,1,0:T(8,128)}, f32[32,128,128]{2,1,0:T(8,128)}) custom-call(f32[3,8,32,256]{3,2,1,0:T(8,128)} %get-tuple-element.6.refs_0_, f32[8,32,256]{2,1,0:T(8,128)} %get-tuple-element.7.refs_1_, f32[32,128,128]{2,1,0:T(8,128)} %get-tuple-element.8.refs_2_), custom_call_target="tpu_custom_call" | custom-call | tf_op jit(solution)/shard_map/store/pallas_call | solution.py:765
